TPU v7x, 256 devices: a whole 4x4x8 slice. The times are simulated.
256 devices in a mesh: group: 2 (over z_hi), resp: 16 (over y, z_lo), tp: 8 (over x, core).
Axes of the slice: x: 4, y: 4, z: 8 (z_hi: 2, z_lo: 4; z = z_hi * 4 + z_lo), core: 2. Of those that a mesh axis runs over, the one named last changes fastest.
Arguments:
- queries: bfloat16 [4096, 8192], P(('group', 'resp'), 'tp'), parts along dimension 0, may hold values from -8 to 8
- prompt_keys: bfloat16 [8192, 1024], P(('group', 'resp'), 'tp'), parts along dimension 0, may hold values from -8 to 8
- prompt_values: bfloat16 [8192, 1024], P(('group', 'resp'), 'tp'), parts along dimension 0, may hold values from -6 to 6
- resp_keys: bfloat16 [4096, 1024], P(('group', 'resp'), 'tp'), parts along dimension 0, may hold values from -6 to 6
- resp_values: bfloat16 [4096, 1024], P(('group', 'resp'), 'tp'), parts along dimension 0, may hold values from -6 to 6
- grad_out: bfloat16 [4096, 8192], P(('group', 'resp'), 'tp'), parts along dimension 0, may hold values from -24 to 24
- lengths: int32 [32], P(('group', 'resp')), parts along dimension 0, may hold values from 32 to 128, as said below
Outputs:
- grad_queries: bfloat16 [4096, 8192], P(('group', 'resp'), 'tp'), parts along dimension 0
- grad_prompt_keys: bfloat16 [8192, 1024], P(('group', 'resp'), 'tp'), parts along dimension 0
- grad_prompt_values: bfloat16 [8192, 1024], P(('group', 'resp'), 'tp'), parts along dimension 0
- grad_resp_keys: bfloat16 [4096, 1024], P(('group', 'resp'), 'tp'), parts along dimension 0
- grad_resp_values: bfloat16 [4096, 1024], P(('group', 'resp'), 'tp'), parts along dimension 0
There are 2 independent parts, one for each index of `group`. A program takes and returns all parts, laid end to end along the dimension named above; each array names one. Nothing has to cross between parts.
Inputs may be any that keep to these rules, and one draw needn't show every extreme that they name: `lengths`: some response has all 128 tokens live.
All inputs are finite; a program needn't handle non-finite values.
Results may differ from a plain program's by a relative error of at most 0.023.
Values may be sent and summed in bfloat16 or wider, within the bound.
No kernel may reach another device: no remote copies, remote signals or barrier semaphores. Data moves between devices by JAX's collectives and lax.ppermute only.
A program may use at most 64 MiB of HBM per device.

v0:
```python
import math

import jax
import jax.numpy as jnp
from jax import lax
from jax.sharding import PartitionSpec as P

HEADS = 64
KV_HEADS = 8
HEAD_DIM = 128


def body(queries, prompt_keys, prompt_values, resp_keys, resp_values, grad_out, lengths):
    seq_len = queries.shape[0]
    local_heads = resp_keys.shape[1] // HEAD_DIM
    group_size = HEADS // KV_HEADS
    scaling = HEAD_DIM ** (-0.5)
    query_rows = queries.reshape(seq_len, local_heads, group_size, HEAD_DIM)
    row_index = jnp.arange(seq_len)[:, None]
    col_index = jnp.arange(seq_len)[None, :]
    causal = col_index <= row_index

    def block_scores(keys_block, masking):
        shaped = keys_block.reshape(-1, local_heads, HEAD_DIM)
        scores = (
            jnp.einsum("lkge,bke->kglb", query_rows, shaped, preferred_element_type=jnp.float32)
            * scaling
        )
        if masking:
            scores = jnp.where(causal[None, None], scores, -jnp.inf)
        return scores

    def absorb(state, keys_block, values_block, masking):
        highest, totals, attended = state
        scores = block_scores(keys_block, masking)
        newest = jnp.maximum(highest, jnp.max(scores, -1))
        factor = jnp.exp(highest - newest)
        exps = jnp.exp(scores - newest[..., None])
        totals = totals * factor + jnp.sum(exps, -1)
        shaped = values_block.reshape(-1, local_heads, HEAD_DIM)
        product = jnp.einsum(
            "kglb,bke->kgle", exps.astype(jnp.bfloat16), shaped, preferred_element_type=jnp.float32
        )
        attended = attended * factor[..., None] + product
        return (newest, totals, attended)

    initial = (
        jnp.full((local_heads, group_size, seq_len), -jnp.inf, jnp.float32),
        jnp.zeros((local_heads, group_size, seq_len), jnp.float32),
        jnp.zeros((local_heads, group_size, seq_len, HEAD_DIM), jnp.float32),
    )
    state = initial
    keys_all = lax.all_gather(prompt_keys, "resp", axis=0, tiled=True)
    values_all = lax.all_gather(prompt_values, "resp", axis=0, tiled=True)
    rows = keys_all.shape[0]
    width = math.gcd(rows, 512)
    count = rows // width

    def advance(carry, items):
        return (absorb(carry, items[0], items[1], False), None)

    stacked = (
        keys_all.reshape(count, width, keys_all.shape[1]),
        values_all.reshape(count, width, values_all.shape[1]),
    )
    state, unused = lax.scan(advance, state, stacked)
    state = absorb(state, resp_keys, resp_values, True)
    highest, totals, attended = state
    attended = (attended / totals[..., None]).astype(jnp.bfloat16)
    live = (jnp.arange(seq_len) < lengths[0]).astype(jnp.bfloat16)
    masked = (grad_out * live[:, None]).reshape(seq_len, local_heads, group_size, HEAD_DIM)
    delta = jnp.einsum("lkge,kgle->kgl", masked, attended, preferred_element_type=jnp.float32)

    def backward_block(keys_block, values_block, masking):
        scores = block_scores(keys_block, masking)
        probs = jnp.exp(scores - highest[..., None]) / totals[..., None]
        keys_shaped = keys_block.reshape(-1, local_heads, HEAD_DIM)
        values_shaped = values_block.reshape(-1, local_heads, HEAD_DIM)
        dprob = jnp.einsum(
            "lkge,bke->kglb", masked, values_shaped, preferred_element_type=jnp.float32
        )
        dscore = (probs * (dprob - delta[..., None])).astype(jnp.bfloat16)
        query_part = jnp.einsum(
            "kglb,bke->lkge", dscore, keys_shaped, preferred_element_type=jnp.float32
        )
        key_term = (
            jnp.einsum("kglb,lkge->bke", dscore, query_rows, preferred_element_type=jnp.float32)
            * scaling
        )
        value_term = jnp.einsum(
            "kglb,lkge->bke", probs.astype(jnp.bfloat16), masked, preferred_element_type=jnp.float32
        )
        rows = keys_block.shape[0]
        return (query_part, key_term.reshape(rows, -1), value_term.reshape(rows, -1))

    keys_all, values_all = (
        lax.all_gather(prompt_keys, "resp", axis=0, tiled=True),
        lax.all_gather(prompt_values, "resp", axis=0, tiled=True),
    )
    total_rows = keys_all.shape[0]
    key_cols = keys_all.shape[1]
    width = math.gcd(total_rows, 512)
    count = total_rows // width
    start_grad = jnp.zeros((seq_len, local_heads, group_size, HEAD_DIM), jnp.float32)
    stacked = (
        keys_all.reshape(count, width, key_cols),
        values_all.reshape(count, width, values_all.shape[1]),
    )

    def backward_step(carry, items):
        query_part, key_term, value_term = backward_block(items[0], items[1], False)
        return (carry + query_part, (key_term, value_term))

    query_grad, (key_terms, value_terms) = lax.scan(backward_step, start_grad, stacked)
    key_terms = key_terms.reshape(total_rows, -1)
    value_terms = value_terms.reshape(total_rows, -1)
    summed_keys, summed_values = (
        lax.psum_scatter(
            key_terms.astype(jnp.bfloat16), "resp", scatter_dimension=0, tiled=True
        ).astype(jnp.float32),
        lax.psum_scatter(
            value_terms.astype(jnp.bfloat16), "resp", scatter_dimension=0, tiled=True
        ).astype(jnp.float32),
    )
    resp_part, resp_key_grad, resp_value_grad = backward_block(resp_keys, resp_values, True)
    grad_queries = (scaling * (query_grad + resp_part)).astype(jnp.bfloat16).reshape(seq_len, -1)
    return (
        grad_queries,
        summed_keys.astype(jnp.bfloat16),
        summed_values.astype(jnp.bfloat16),
        resp_key_grad.astype(jnp.bfloat16),
        resp_value_grad.astype(jnp.bfloat16),
    )


def solution(mesh):
    return jax.shard_map(
        body,
        mesh=mesh,
        in_specs=(
            P(("group", "resp"), "tp"),
            P(("group", "resp"), "tp"),
            P(("group", "resp"), "tp"),
            P(("group", "resp"), "tp"),
            P(("group", "resp"), "tp"),
            P(("group", "resp"), "tp"),
            P(("group", "resp")),
        ),
        out_specs=(
            P(("group", "resp"), "tp"),
            P(("group", "resp"), "tp"),
            P(("group", "resp"), "tp"),
            P(("group", "resp"), "tp"),
            P(("group", "resp"), "tp"),
        ),
        check_vma=False,
    )
```

profile of v0, /device:TPU:2, one launch (start us, length us, event | category | flops | bytes accessed | tf_op | source)
XLA Modules:
  0.0 432.9 jit_solution(17359559391505116813)
XLA Ops:
  9.4 1.1 copy.34
  10.8 1.1 copy.31
  12.4 82.4 %all-gather.3.cloned.1.call-done = bf16[4096,128]{1,0:T(8,128)(2,1)} async-done(((bf16[256,128]{1,0:T(8,128)(2,1)}), bf16[4096,128]{1,0:T(8,128)(2,1)}) %all-gather.3.cloned.1.call-update) | async-done | bytes 1048592 | tf_op jit(solution)/shard_map/all_gather | solution.py:97
  94.8 82.5 %all-gather.5.cloned.1.call-done = bf16[4096,128]{1,0:T(8,128)(2,1)} async-done(((bf16[256,128]{1,0:T(8,128)(2,1)}), bf16[4096,128]{1,0:T(8,128)(2,1)}) %all-gather.5.cloned.1.call-update) | async-done | bytes 1048592 | tf_op jit(solution)/shard_map/all_gather | solution.py:98
  177.3 26.5 %while.30 = (s32[]{:T(128)}, f32[1,8,128]{2,1,0:T(8,128)S(1)}, f32[1,8,128]{2,1,0:T(8,128)S(1)}, f32[1,8,128,128]{3,2,1,0:T(8,128)S(1)}, bf16[8,512,128]{2,1,0:T...) while((s32[]{:T(128)}, f32[1,8,128]{2,1,0:T(8,128)S(1)}, ...), condition=%wide.region_3.4_spmd.clone, body=%wide.region_0.3_spmd.clone.sunk | while | flops 273029120 | bytes 7929977 | solution.py:66
  177.3 1.3 bitcast_reduce_fusion.2
  179.0 1.5 fusion.114
  180.6 1.3 bitcast_reduce_fusion.2
  182.3 1.5 fusion.114
  183.9 1.3 bitcast_reduce_fusion.2
  185.7 1.5 fusion.114
  187.2 1.3 bitcast_reduce_fusion.2
  189.0 1.5 fusion.114
  190.6 1.3 bitcast_reduce_fusion.2
  192.3 1.5 fusion.114
  193.9 1.3 bitcast_reduce_fusion.2
  195.6 1.5 fusion.114
  197.2 1.3 bitcast_reduce_fusion.2
  198.9 1.5 fusion.114
  200.5 1.3 bitcast_reduce_fusion.2
  202.3 1.5 fusion.114
  204.5 50.4 %while.31 = (s32[]{:T(128)}, f32[128,1,8,128]{0,3,2,1:T(8,128)S(1)}, bf16[8,512,128]{2,1,0:T(8,128)(2,1)}, bf16[8,512,128]{2,1,0:T(8,128)(2,1)}, bf16[8,512,128]...) while((s32[]{:T(128)}, ...), condition=%wide.region_7.8_spmd.clone, body=%wide.region_6.7_spmd.clone.sunk | while | flops 675086336 | bytes 12464291 | solution.py:114
  204.5 1.4 fusion.125
  205.9 1.3 fusion.126
  207.3 1.1 fusion.129
  208.4 1.3 fusion.127
  209.7 1.1 fusion.128
  210.8 1.4 fusion.125
  212.2 1.3 fusion.126
  213.6 1.1 fusion.129
  214.7 1.3 fusion.127
  216.0 1.1 fusion.128
  217.1 1.4 fusion.125
  218.5 1.3 fusion.126
  219.9 1.1 fusion.129
  221.0 1.3 fusion.127
  222.3 1.1 fusion.128
  223.4 1.4 fusion.125
  224.8 1.3 fusion.126
  226.2 1.1 fusion.129
  227.3 1.3 fusion.127
  228.6 1.1 fusion.128
  229.7 1.4 fusion.125
  231.2 1.3 fusion.126
  232.5 1.1 fusion.129
  233.6 1.3 fusion.127
  234.9 1.1 fusion.128
  236.0 1.4 fusion.125
  237.4 1.3 fusion.126
  238.8 1.1 fusion.129
  239.9 1.3 fusion.127
  241.2 1.1 fusion.128
  242.3 1.4 fusion.125
  243.7 1.3 fusion.126
  245.1 1.1 fusion.129
  246.2 1.3 fusion.127
  247.5 1.1 fusion.128
  248.6 1.4 fusion.125
  250.0 1.3 fusion.126
  251.4 1.1 fusion.129
  252.5 1.3 fusion.127
  253.8 1.1 fusion.128
  258.7 82.0 %reduce-scatter.5.cloned.1.call-done = bf16[256,128]{1,0:T(8,128)(2,1)} async-done(((bf16[4096,128]{1,0:T(8,128)(2,1)}), bf16[256,128]{1,0:T(8,128)(2,1)}) %reduce-scatter.5.cloned.1.call-update) | async-done | bytes 65552 | tf_op jit(solution)/shard_map/reduce_scatter | solution.py:121
  340.7 85.7 %reduce-scatter.3.cloned.1.call-done = bf16[256,128]{1,0:T(8,128)(2,1)} async-done(((bf16[4096,128]{1,0:T(8,128)(2,1)}), bf16[256,128]{1,0:T(8,128)(2,1)}) %reduce-scatter.3.cloned.1.call-update) | async-done | bytes 65552 | tf_op jit(solution)/shard_map/reduce_scatter | solution.py:118
  (69 shorter events, 9.5 us)
Async XLA Ops:
  7.2 5.0 %copy-start = (bf16[128,128]{1,0:T(8,128)(2,1)S(1)}, bf16[128,128]{1,0:T(8,128)(2,1)}, u32[]{:S(2)}) copy-start(bf16[128,128]{1,0:T(8,128)(2,1)} %param.14) | copy-start | bytes 98308
  7.2 5.0 %copy-start.1 = (bf16[128,1024]{1,0:T(8,128)(2,1)S(1)}, bf16[128,1024]{1,0:T(8,128)(2,1)}, u32[]{:S(2)}) copy-start(bf16[128,1024]{1,0:T(8,128)(2,1)} %param.11) | copy-start | bytes 786436
  7.2 87.6 %all-gather.3.cloned.1.call-start = ((), (), s32[]{:S(2)}) async-start(), calls=%async_computation.2 | async-start | bytes 1114112 | tf_op jit(solution)/shard_map/all_gather | solution.py:97
  7.9 169.4 %all-gather.5.cloned.1.call-start = ((), (), s32[]{:S(2)}) async-start(), calls=%async_computation.3 | async-start | bytes 1114112 | tf_op jit(solution)/shard_map/all_gather | solution.py:98
  8.7 332.0 %reduce-scatter.5.cloned.1.call-start = ((), (), s32[]{:S(2)}) async-start(), calls=%async_computation.5 | async-start | bytes 1114112 | tf_op jit(solution)/shard_map/reduce_scatter | solution.py:121
  177.3 26.9 %copy-start.2 = (bf16[128,128]{1,0:T(8,128)(2,1)S(1)}, bf16[128,128]{1,0:T(8,128)(2,1)}, u32[]{:S(2)}) copy-start(bf16[128,128]{1,0:T(8,128)(2,1)} %param.15) | copy-start | bytes 98308
  254.9 171.4 %reduce-scatter.3.cloned.1.call-start = ((), (), s32[]{:S(2)}) async-start(), calls=%async_computation.4 | async-start | bytes 1114112 | tf_op jit(solution)/shard_map/reduce_scatter | solution.py:118
Sparse Core Ops, SparseCore 0:
  9.8 84.9 all-gather.2
  96.6 80.6 all-gather.4
  255.0 85.5 reduce-scatter.4
  343.8 82.5 reduce-scatter.2
where the time goes:
time: 434 us; the launch traced here: 433 us
  waiting for transfers between devices  334 us (77%)
  matrix products  75.4 us (17%)
  between operations  14.6 us (3%)
  local copies, waits for them, and re-layouts  4.41 us (1%)
    reduce_scatter x1, waiting for transfers between devices, body(): lax.psum_scatter(key_terms.astype(jnp.bfloat16), 'resp', scatter_dimensio...  85.7 us
    all_gather x1, waiting for transfers between devices, body(): lax.all_gather(prompt_values, 'resp', axis=0, tiled=True)  82.5 us
    all_gather x1, waiting for transfers between devices, body(): lax.all_gather(prompt_keys, 'resp', axis=0, tiled=True)  82.4 us
    reduce_scatter x1, waiting for transfers between devices, body(): lax.psum_scatter(value_terms.astype(jnp.bfloat16), 'resp', scatter_dimens...  82 us
    dot_general x17, matrix products, block_scores(): jnp.einsum('lkge,bke->kglb', query_rows, shaped, preferred_element_type=j...  22.5 us
    dot_general x9, matrix products, absorb(): jnp.einsum('kglb,bke->kgle', exps.astype(jnp.bfloat16), shaped, preferred...  12.6 us
    dot_general x9, matrix products, backward_block(): jnp.einsum('lkge,bke->kglb', masked, values_shaped, preferred_element_typ...  11 us
    dot_general x9, matrix products, backward_block(): jnp.einsum('kglb,bke->lkge', dscore, keys_shaped, preferred_element_type=...  10.7 us
  transfers between devices with their start and end apart: 4, of which 4 were waited for; matrix products, arithmetic and copies ran while one was open for 1% of the time, Pallas kernels for 0%

commit v1 on v0

v1 whole, which is shorter than its diff:
```python
import functools

import jax
import jax.numpy as jnp
from jax import lax
from jax.experimental import pallas as pl
from jax.experimental.pallas import tpu as pltpu
from jax.sharding import PartitionSpec as P

HEAD_DIM = 128
SIDE = 4
LOG2E = 1.4426950408889634
BF16 = jnp.bfloat16
F32 = jnp.float32


def dot(a, b, ca, cb):
    return lax.dot_general(a, b, (((ca,), (cb,)), ((), ())), preferred_element_type=F32)


def stack_heads(q_ref):
    heads = q_ref.shape[1] // HEAD_DIM
    return jnp.concatenate([q_ref[:, h * HEAD_DIM : (h + 1) * HEAD_DIM] for h in range(heads)], 0)


def prepare_kernel(len_hbm, q_hbm, g_hbm, k_hbm, v_hbm, kr_hbm, vr_hbm,
                   mt_ref, q_ref, kv_ref, kr_ref, vr_ref, g_ref, len_ref, sems):
    piece = k_hbm.shape[0]
    pairs = (
        (len_hbm, len_ref),
        (g_hbm, g_ref),
        (k_hbm, kv_ref.at[pl.ds(0, piece)]),
        (v_hbm, kv_ref.at[pl.ds(piece, piece)]),
        (q_hbm, q_ref),
        (kr_hbm, kr_ref),
        (vr_hbm, vr_ref),
    )
    copies = [pltpu.make_async_copy(a, b, sems.at[n]) for n, (a, b) in enumerate(pairs)]
    for copy in copies:
        copy.start()
    copies[0].wait()
    copies[1].wait()
    rows, cols = g_ref.shape
    alive = lax.broadcasted_iota(jnp.int32, (rows, cols), 0) < len_ref[0]
    masked = jnp.where(alive, g_ref[...].astype(F32), 0.0)
    for h in range(cols // HEAD_DIM):
        part = masked[:, h * HEAD_DIM : (h + 1) * HEAD_DIM]
        mt_ref[:, h * rows : (h + 1) * rows] = part.T.astype(BF16)
    for copy in copies[2:]:
        copy.wait()


def plane_of(pieces, part):
    size = pieces[0].shape[0] // 2
    return jnp.concatenate([p[part * size : (part + 1) * size, :] for p in pieces], 0)


def score_block(s_ref, base, keys, q, highest, mask=None):
    group = highest.shape[0]
    step = min(256, keys.shape[0])
    for r in range(0, keys.shape[0], step):
        s = dot(keys[r : r + step, :], q, 1, 1)
        if mask is not None:
            s = jnp.where(mask, s, -jnp.inf)
        s_ref[base + r : base + r + step, :] = s
        highest = jnp.maximum(highest, jnp.max(s.reshape(step // group, group, s.shape[1]), 0))
    return highest


def weigh(s_ref, w_ref, highest):
    group, step = 16, 64
    scale = HEAD_DIM**-0.5 * LOG2E
    totals = jnp.zeros((group, s_ref.shape[1]), F32)
    for r in range(0, s_ref.shape[0], step):
        w = jnp.exp2((s_ref[r : r + step, :] - highest) * scale)
        w_ref[r : r + step, :] = w.astype(BF16)
        totals = totals + jnp.sum(w.reshape(step // group, group, w.shape[1]), 0)
    return jnp.sum(totals, 0, keepdims=True)


def summary(highest, totals, attended, n, high_ref, lse_ref, a_ref):
    high = highest * (HEAD_DIM**-0.5 * LOG2E)
    high_ref[n : n + 1, :] = high
    lse_ref[n : n + 1, :] = high + jnp.log2(totals)
    a_ref[...] = attended / totals


def own_kernel(q_ref, kr, vr, p0, p1, p2, p3, w_ref, high_ref, lse_ref, a_ref, s_ref):
    rows = kr.shape[0]
    wide = w_ref.shape[1]
    pieces = (p0, p1, p2, p3)
    q = stack_heads(q_ref)
    key_pos = lax.broadcasted_iota(jnp.int32, (rows, wide), 0)
    token = lax.broadcasted_iota(jnp.int32, (rows, wide), 1) % rows
    highest = jnp.full((16, wide), -jnp.inf, F32)
    highest = score_block(s_ref, 0, kr, q, highest, key_pos <= token)
    highest = score_block(s_ref, rows, plane_of(pieces, 0), q, highest)
    highest = jnp.max(highest, 0, keepdims=True)
    totals = weigh(s_ref, w_ref, highest)
    attended = dot(vr[...], w_ref[0:rows, :], 0, 0) + dot(
        plane_of(pieces, 1), w_ref[rows:, :], 0, 0
    )
    summary(highest, totals, attended, 0, high_ref, lse_ref, a_ref)


def other_kernel(q1, q2, q3, p0, p1, p2, p3, w1, w2, w3, high_ref, lse_ref, a1, a2, a3, s1, s2, s3):
    pieces = (p0, p1, p2, p3)
    keys, values = plane_of(pieces, 0), plane_of(pieces, 1)
    for n, (q, w, a, s_ref) in enumerate(((q1, w1, a1, s1), (q2, w2, a2, s2), (q3, w3, a3, s3))):
        highest = jnp.full((16, w.shape[1]), -jnp.inf, F32)
        highest = score_block(s_ref, 0, keys, stack_heads(q), highest)
        highest = jnp.max(highest, 0, keepdims=True)
        totals = weigh(s_ref, w, highest)
        summary(highest, totals, dot(values, w[...], 0, 0), n, high_ref, lse_ref, a)


def delta_kernel(high0, high123, lse0, lse123, a0, a1, a2, a3, m0, m1, m2, m3, high_ref, stat_ref):
    high_ref[0:1, :] = high0[...]
    high_ref[1:SIDE, :] = high123[...]
    stat_ref[0:1, :] = lse0[...]
    for d, (a, m) in enumerate(zip((a0, a1, a2, a3), (m0, m1, m2, m3))):
        if d:
            stat_ref[2 * d : 2 * d + 1, :] = lse123[d - 1 : d, :]
        part = jnp.sum(m[...].astype(F32) * a[...], 0, keepdims=True)
        stat_ref[2 * d + 1 : 2 * d + 2, :] = part


def product_kernel(stat_ref, p0, p1, p2, p3, vr, m0, m1, m2, m3, x0, x1, x2, x3, xr):
    values = plane_of((p0, p1, p2, p3), 1)
    for m, x in ((m1, x1), (m3, x3), (m2, x2), (m0, x0)):
        x[...] = dot(values, m[...], 1, 0)
    xr[...] = dot(vr[...], m0[...], 1, 0)


def settle(stats, high_ref, d):
    parts = []
    for e, ref in enumerate(stats):
        row = 2 * ((d - e) % SIDE)
        parts.append((ref[row : row + 1, :], ref[row + 1 : row + 2, :]))
    highest = parts[0][0]
    for lse, term in parts[1:]:
        highest = jnp.maximum(highest, lse)
    totals = jnp.zeros_like(highest)
    delta = jnp.zeros_like(highest)
    for lse, term in parts:
        share = jnp.exp2(lse - highest)
        totals = totals + share
        delta = delta + term * share
    return jnp.exp2(high_ref[d : d + 1, :] - highest) / totals, delta / totals


def turn_back(total, out):
    rows = out.shape[0]
    total = total * HEAD_DIM**-0.5
    for h in range(total.shape[1] // rows):
        part = total[:, h * rows : (h + 1) * rows]
        out[:, h * HEAD_DIM : (h + 1) * HEAD_DIM] = part.T.astype(BF16)


def remote_kernel(t0, t1, t2, t3, high_ref, p0, p1, p2, p3, w2, x2,
                  factor_ref, delta_ref, q2, ds2):
    stats = (t0, t1, t2, t3)
    for d in range(SIDE):
        factor, delta = settle(stats, high_ref, d)
        factor_ref[d : d + 1, :] = factor
        delta_ref[d : d + 1, :] = delta
        if d == 2:
            ds = w2[...] * ((x2[...] - delta) * factor).astype(BF16)
            ds2[...] = ds
            turn_back(dot(plane_of((p0, p1, p2, p3), 0), ds, 0, 0), q2)


def local_kernel(factor_ref, delta_ref, p0, p1, p2, p3, kr, w0, w1, w2, w3, x0, x1, x3, xr, ds2,
                 m0, m1, m2, m3, q0, q1, q2, q3, dq0, dq1, dq3, dkr_ref, dvr_ref, o0, o1, o2, o3):
    rows = kr.shape[0]
    size = p0.shape[0] // 2
    scale = HEAD_DIM**-0.5
    plane_keys = plane_of((p0, p1, p2, p3), 0)

    def pair(d):
        return factor_ref[d : d + 1, :], delta_ref[d : d + 1, :]

    def masked(m, d):
        return (m[...].astype(F32) * factor_ref[d : d + 1, :]).astype(BF16)

    keys = dot(ds2[...], stack_heads(q2), 1, 0)
    values = dot(w2[...], masked(m2, 2), 1, 1)
    for d, q, m, w, x, out in ((1, q1, m1, w1, x1, dq1), (3, q3, m3, w3, x3, dq3)):
        factor, delta = pair(d)
        ds = w[...] * ((x[...] - delta) * factor).astype(BF16)
        turn_back(dot(plane_keys, ds, 0, 0), out)
        keys = keys + dot(ds, stack_heads(q), 1, 0)
        values = values + dot(w[...], masked(m, d), 1, 1)
    factor, delta = pair(0)
    q = stack_heads(q0)
    g = masked(m0, 0)
    near = w0[0:rows, :]
    ds = near * ((xr[...] - delta) * factor).astype(BF16)
    dvr_ref[...] = dot(near, g, 1, 1).astype(BF16)
    dkr_ref[...] = (dot(ds, q, 1, 0) * scale).astype(BF16)
    grad = dot(kr[...], ds, 0, 0)
    ds = w0[rows:, :] * ((x0[...] - delta) * factor).astype(BF16)
    turn_back(grad + dot(plane_keys, ds, 0, 0), dq0)
    keys = ((keys + dot(ds, q, 1, 0)) * scale).astype(BF16)
    values = (values + dot(w0[rows:, :], g, 1, 1)).astype(BF16)
    for d, out in enumerate((o0, o1, o2, o3)):
        out[0:size, :] = keys[d * size : (d + 1) * size, :]
        out[size : 2 * size, :] = values[d * size : (d + 1) * size, :]


def shift_y(d):
    return [(y * SIDE + z, (y + d) % SIDE * SIDE + z) for y in range(SIDE) for z in range(SIDE)]


def shift_z(d):
    return [(y * SIDE + z, y * SIDE + (z + d) % SIDE) for y in range(SIDE) for z in range(SIDE)]


def send(x, perm):
    return lax.ppermute(x, "resp", perm)


def combine(own, received):
    own = own.astype(F32)
    for x in received:
        own = own + x.astype(F32)
    return own.astype(BF16)


def from_others(x, shift):
    one, three, two = (send(x, shift(d)) for d in (1, 3, 2))
    return one, two, three


def call(kernel, name, outs, inputs, memory, scratch=(), flops=0, exps=0, space=pltpu.VMEM):
    return pl.pallas_call(
        kernel,
        out_shape=[jax.ShapeDtypeStruct(*o) for o in outs],
        in_specs=[pl.BlockSpec(memory_space=space)] * len(inputs),
        out_specs=[pl.BlockSpec(memory_space=pltpu.VMEM)] * len(outs),
        scratch_shapes=list(scratch),
        compiler_params=pltpu.CompilerParams(vmem_limit_bytes=memory * 2**20),
        cost_estimate=pl.CostEstimate(flops=flops, bytes_accessed=2**20, transcendentals=exps),
        name=name,
    )(*inputs)


def body(queries, prompt_keys, prompt_values, resp_keys, resp_values, grad_out, lengths):
    rows, cols = queries.shape
    part = prompt_keys.shape[0]
    plane = SIDE * part
    wide = rows * cols // HEAD_DIM
    near = plane + rows
    unit = 2 * wide * plane * HEAD_DIM
    turned = ((HEAD_DIM, wide), BF16)
    turned_wide = ((HEAD_DIM, wide), F32)
    small = ((rows, HEAD_DIM), BF16)
    flat = ((rows, cols), BF16)
    both = ((2 * part, HEAD_DIM), BF16)
    square = ((plane, wide), BF16)
    square_wide = ((plane, wide), F32)
    scores = pltpu.VMEM((plane, wide), F32)

    q1, q3 = (send(queries, shift_y(d)) for d in (1, 3))
    q2 = send(q1, shift_y(1))
    params = (queries, grad_out, prompt_keys, prompt_values, resp_keys, resp_values)
    m0, q0, piece, kr, vr = call(
        prepare_kernel, "prepare", [turned, flat, both, small, small],
        [lengths] + [pltpu.with_memory_space_constraint(x, pltpu.HBM) for x in params], 8,
        [pltpu.VMEM((rows, cols), BF16), pltpu.SMEM((1,), jnp.int32),
         pltpu.SemaphoreType.DMA((7,))], space=pltpu.HBM)
    p1, p3 = (send(piece, shift_z(d)) for d in (1, 3))
    pieces = (piece, p1, send(p1, shift_z(1)), p3)
    m1, m3 = (send(m0, shift_y(d)) for d in (1, 3))
    m2 = send(m3, shift_y(3))
    w0, high0, lse0, a0 = call(
        own_kernel, "own", [((near, wide), BF16), ((1, wide), F32), ((1, wide), F32), turned_wide],
        (q0, kr, vr, *pieces), 16, [pltpu.VMEM((near, wide), F32)],
        flops=2 * unit, exps=near * wide)
    w1, w2, w3, high, lse, a1, a2, a3 = call(
        other_kernel, "other",
        [square] * 3 + [((SIDE - 1, wide), F32)] * 2 + [turned_wide] * 3,
        (q1, q2, q3, *pieces), 28, [scores] * 3, flops=6 * unit, exps=3 * plane * wide)
    high, stat = call(
        delta_kernel, "delta", [((SIDE, wide), F32), ((2 * SIDE, wide), F32)],
        (high0, high, lse0, lse, a0, a1, a2, a3, m0, m1, m2, m3), 8, flops=unit // 2)
    all_stats = (stat, *from_others(stat, shift_y))
    x0, x1, x2, x3, xr = call(
        product_kernel, "product", [square_wide] * 4 + [((rows, wide), F32)],
        (stat, *pieces, vr, m0, m1, m2, m3), 12, flops=4 * unit)
    factors, delta, dq2, ds2 = call(
        remote_kernel, "remote",
        [((SIDE, wide), F32)] * 2 + [flat, square],
        (*all_stats, high, *pieces, w2, x2), 12, flops=unit)
    back2 = send(dq2, shift_y(-2))
    dq0, dq1, dq3, dkr, dvr, o0, o1, o2, o3 = call(
        local_kernel, "local", [flat] * 3 + [small, small] + [both] * 4,
        (factors, delta, *pieces, kr, w0, w1, w2, w3, x0, x1, x3, xr, ds2,
         m0, m1, m2, m3, q0, q1, q2, q3), 16, flops=11 * unit)
    o2, unused = lax.optimization_barrier((o2, back2))
    total = combine(o0, [send(x, shift_z(-d)) for d, x in ((1, o1), (3, o3), (2, o2))])
    returned = [send(x, shift_y(-d)) for d, x in ((1, dq1), (3, dq3))] + [back2]
    grad_queries = combine(dq0, returned)
    return grad_queries, total[:part], total[part:], dkr, dvr


def solution(mesh):
    spec = P(("group", "resp"), "tp")
    return jax.shard_map(
        body,
        mesh=mesh,
        in_specs=(spec,) * 6 + (P(("group", "resp")),),
        out_specs=(spec,) * 5,
        check_vma=False,
    )
```

time: 434 us -> 63 us (0.15)
  waiting for transfers between devices: 334 us -> 13.5 us
  matrix products: 75.4 us -> 0 us
  starting transfers between devices: 0.16 us -> 26.6 us
  Pallas kernels: 0 us -> 19.8 us
  between operations: 14.6 us -> 1.38 us
    reduce_scatter x2 -> x0, waiting for transfers between devices: 168 us -> none  [the longest x1 85.7 us: body(): lax.psum_scatter(key_terms.astype(jnp.bfloat16), 'resp', scatter_dimensio...]
    all_gather x2 -> x0, waiting for transfers between devices: 165 us -> none  [the longest x1 82.5 us: body(): lax.all_gather(prompt_values, 'resp', axis=0, tiled=True)]
    dot_general x62 -> x0, matrix products: 75.4 us -> none  [the longest x17 22.5 us: block_scores(): jnp.einsum('lkge,bke->kglb', query_rows, shaped, preferred_element_type=j...]
    ppermute x0 -> x18, starting transfers between devices: none -> 26.6 us  [send(): return lax.ppermute(x, 'resp', perm)]
    pallas_call x0 -> x7, Pallas kernels: none -> 19.8 us  [call(): pl.pallas_call(kernel, out_shape=[jax.ShapeDtypeStruct(*o) for o in outs]...]
    ppermute x0 -> x18, waiting for transfers between devices: none -> 13.5 us  [send(): return lax.ppermute(x, 'resp', perm)]
  transfers between devices with their start and end apart: 4 -> 18, of which waited for: 4 -> 9; matrix products, arithmetic and copies ran while one was open for 1% -> 1% of each run, Pallas kernels for 0% -> 29%
where the time goes in v1:
time: 63 us; the launch traced here: 62.9 us
  starting transfers between devices  26.6 us (42%)
  Pallas kernels  19.8 us (31%)
  waiting for transfers between devices  13.5 us (21%)
  between operations  1.38 us (2%)
  other arithmetic  0.94 us (1%)
  local copies, waits for them, and re-layouts  0.66 us (1%)
    ppermute x18, starting transfers between devices, send(): return lax.ppermute(x, 'resp', perm)  26.6 us
    pallas_call x7, Pallas kernels, call(): pl.pallas_call(kernel, out_shape=[jax.ShapeDtypeStruct(*o) for o in outs]...  19.8 us
    ppermute x18, waiting for transfers between devices, send(): return lax.ppermute(x, 'resp', perm)  13.5 us
  transfers between devices with their start and end apart: 18, of which 9 were waited for; matrix products, arithmetic and copies ran while one was open for 1% of the time, Pallas kernels for 29%

profile of v1, /device:TPU:2, one launch (start us, length us, event | category | flops | bytes accessed | tf_op | source)
XLA Modules:
  0.0 62.9 jit_solution(699976863961460806)
XLA Ops:
  0.6 1.7 %collective-permute-start.3 = (bf16[128,1024]{1,0:T(8,128)(2,1)}, bf16[128,1024]{1,0:T(8,128)(2,1)S(1)}, u32[]{:S(2)}, u32[]{:S(2)}) collective-permute-start(bf16[128,1024]{1,0:T(8,128)(2,1)} %q_hbm.1), channel_id=1, source_target_pairs={{0,32},{8,40},{16,48},{24,56},{32,64},{40,72},{48,80},{56,88},{64,... | collective-permute-start | bytes 786440 | tf_op jit(solution)/shard_map/ppermute | solution.py:220
  2.9 1.2 %prepare.1 = (bf16[128,1024]{1,0:T(8,128)(2,1)S(1)}, bf16[128,1024]{1,0:T(8,128)(2,1)S(1)}, bf16[512,128]{1,0:T(8,128)(2,1)S(1)}, bf16[128,128]{1,0:T(8,128)(2,1)S(1)}, bf16[128,128]{1,0:T(8,128)(2,1)S(1)}) custom-call(s32[1]{0:T(128)S(6)} %copy.12.len_hbm, bf16[128,1024]{1,0:T(8,128)(2,1)} %q_hbm.1, bf16[128,1024]{1,0:T(8,128)(2,1)} %g_hbm.1, ...), custom_call_target="tpu_custom_call" | custom-call | bytes 1048576 | tf_op jit(solution)/shard_map/prepare/pallas_call | solution.py:236
  4.1 1.7 %collective-permute-start.7 = (bf16[128,1024]{1,0:T(8,128)(2,1)S(1)}, bf16[128,1024]{1,0:T(8,128)(2,1)S(1)}, u32[]{:S(2)}, u32[]{:S(2)}) collective-permute-start(bf16[128,1024]{1,0:T(8,128)(2,1)S(1)} %get-tuple-element.55.m0), channel_id=1, source_target_pairs={{0,96},{8,104},{16,112},{24,120},{32,0},{40,8},{48,16},{56,24},{64... | collective-permute-start | bytes 786440 | tf_op jit(solution)/shard_map/ppermute | solution.py:220
  5.8 1.9 %collective-permute-start = (bf16[512,128]{1,0:T(8,128)(2,1)S(1)}, bf16[512,128]{1,0:T(8,128)(2,1)S(1)}, u32[]{:S(2)}, u32[]{:S(2)}) collective-permute-start(bf16[512,128]{1,0:T(8,128)(2,1)S(1)} %get-tuple-element.46.p0), channel_id=1, source_target_pairs={{0,8},{8,16},{16,24},{24,0},{32,40},{40,48},{48,56},{56,32},{64,72... | collective-permute-start | bytes 393224 | tf_op jit(solution)/shard_map/ppermute | solution.py:220
  7.8 1.8 %collective-permute-start.5 = (bf16[128,1024]{1,0:T(8,128)(2,1)}, bf16[128,1024]{1,0:T(8,128)(2,1)S(1)}, u32[]{:S(2)}, u32[]{:S(2)}) collective-permute-start(bf16[128,1024]{1,0:T(8,128)(2,1)} %q_hbm.1), channel_id=1, source_target_pairs={{0,96},{8,104},{16,112},{24,120},{32,0},{40,8},{48,16},{56,24},{64... | collective-permute-start | bytes 786440 | tf_op jit(solution)/shard_map/ppermute | solution.py:220
  9.6 0.7 %collective-permute-done.3.q1 = bf16[128,1024]{1,0:T(8,128)(2,1)S(1)} collective-permute-done((bf16[128,1024]{1,0:T(8,128)(2,1)}, bf16[128,1024]{1,0:T(8,128)(2,1)S(1)}, u32[]{:S(2)}, u32[]{:S(2)}) %collective-permute-start.3) | collective-permute-done | bytes 262176 | tf_op jit(solution)/shard_map/ppermute | solution.py:220
  10.2 0.3 collective-permute-start.4
  10.5 4.6 %collective-permute-start.2 = (bf16[512,128]{1,0:T(8,128)(2,1)S(1)}, bf16[512,128]{1,0:T(8,128)(2,1)S(1)}, u32[]{:S(2)}, u32[]{:S(2)}) collective-permute-start(bf16[512,128]{1,0:T(8,128)(2,1)S(1)} %get-tuple-element.46.p0), channel_id=1, source_target_pairs={{0,24},{8,0},{16,8},{24,16},{32,56},{40,32},{48,40},{56,48},{64,88... | collective-permute-start | bytes 393224 | tf_op jit(solution)/shard_map/ppermute | solution.py:220
  15.2 0.0 collective-permute-done.p1
  15.2 0.0 collective-permute-start.1
  15.2 3.1 %collective-permute-done.2.p3 = bf16[512,128]{1,0:T(8,128)(2,1)S(1)} collective-permute-done((bf16[512,128]{1,0:T(8,128)(2,1)S(1)}, bf16[512,128]{1,0:T(8,128)(2,1)S(1)}, u32[]{:S(2)}, u32[]{:S(2)}) %collective-permute-start.2) | collective-permute-done | bytes 131104 | tf_op jit(solution)/shard_map/ppermute | solution.py:220
  18.2 1.5 %collective-permute-start.6 = (bf16[128,1024]{1,0:T(8,128)(2,1)S(1)}, bf16[128,1024]{1,0:T(8,128)(2,1)S(1)}, u32[]{:S(2)}, u32[]{:S(2)}) collective-permute-start(bf16[128,1024]{1,0:T(8,128)(2,1)S(1)} %get-tuple-element.55.m0), channel_id=1, source_target_pairs={{0,32},{8,40},{16,48},{24,56},{32,64},{40,72},{48,80},{56,88},{64,... | collective-permute-start | bytes 786440 | tf_op jit(solution)/shard_map/ppermute | solution.py:220
  19.8 0.0 collective-permute-done.7.m3
  19.8 1.7 %collective-permute-start.8 = (bf16[128,1024]{1,0:T(8,128)(2,1)S(1)}, bf16[128,1024]{1,0:T(8,128)(2,1)S(1)}, u32[]{:S(2)}, u32[]{:S(2)}) collective-permute-start(bf16[128,1024]{1,0:T(8,128)(2,1)S(1)} %collective-permute-done.7.m3), channel_id=1, source_target_pairs={{0,96},{8,104},{16,112},{24,120},{32,0},{40,8},{48,16},{56,24},{64... | collective-permute-start | bytes 786440 | tf_op jit(solution)/shard_map/ppermute | solution.py:220
  21.5 0.5 collective-permute-done.1.p2
  21.9 2.2 %own.1 = (bf16[1152,1024]{1,0:T(8,128)(2,1)S(1)}, f32[1,1024]{1,0:T(1,128)S(1)}, f32[1,1024]{1,0:T(1,128)S(1)}, f32[128,1024]{1,0:T(8,128)S(1)}) custom-call(bf16[128,1024]{1,0:T(8,128)(2,1)S(1)} %get-tuple-element.43.q_ref.q0, bf16[128,128]{1,0:T(8,128)(2,1)S(1)} %get-tuple-element.44.kr, bf16[128,128]{1,0:T(8,128)(2,1)S(1)} %get-tuple-element.45.vr, ...), custom_call_target="tpu_custom_call" | custom-call | flops 536870912 | bytes 1048576 | tf_op jit(solution)/shard_map/own/pallas_call | solution.py:236
  24.2 0.0 collective-permute-done.5.q3
  24.2 0.0 collective-permute-done.4.q2
  24.2 5.7 %other.1 = (bf16[1024,1024]{1,0:T(8,128)(2,1)S(1)}, bf16[1024,1024]{1,0:T(8,128)(2,1)S(1)}, bf16[1024,1024]{1,0:T(8,128)(2,1)S(1)}, f32[3,1024]{1,0:T(4,128)S(1)...) custom-call(bf16[128,1024]{1,0:T(8,128)(2,1)S(1)} %collective-permute-don, ...), custom_call_target="tpu_custom_call" | custom-call | flops 1610612736 | bytes 1048576 | tf_op jit(solution)/shard_map/other/pallas_call | solution.py:236
  29.9 0.0 collective-permute-done.6.m1
  29.9 0.0 collective-permute-done.8.m2
  29.9 0.3 delta.1
  30.3 3.0 %collective-permute-start.11 = (f32[8,1024]{1,0:T(8,128)S(1)}, f32[8,1024]{1,0:T(8,128)S(1)}, u32[]{:S(2)}, u32[]{:S(2)}) collective-permute-start(f32[8,1024]{1,0:T(8,128)S(1)} %get-tuple-element.56.stat_ref.t0), channel_id=1, source_target_pairs={{0,96},{8,104},{16,112},{24,120},{32,0},{40,8},{48,16},{56,24},{64... | collective-permute-start | bytes 98312 | tf_op jit(solution)/shard_map/ppermute | solution.py:220
  33.3 0.7 %collective-permute-start.10 = (f32[8,1024]{1,0:T(8,128)S(1)}, f32[8,1024]{1,0:T(8,128)S(1)}, u32[]{:S(2)}, u32[]{:S(2)}) collective-permute-start(f32[8,1024]{1,0:T(8,128)S(1)} %get-tuple-element.56.stat_ref.t0), channel_id=1, source_target_pairs={{0,64},{8,72},{16,80},{24,88},{32,96},{40,104},{48,112},{56,120},{... | collective-permute-start | bytes 98312 | tf_op jit(solution)/shard_map/ppermute | solution.py:220
  34.0 0.7 %collective-permute-start.9 = (f32[8,1024]{1,0:T(8,128)S(1)}, f32[8,1024]{1,0:T(8,128)S(1)}, u32[]{:S(2)}, u32[]{:S(2)}) collective-permute-start(f32[8,1024]{1,0:T(8,128)S(1)} %get-tuple-element.56.stat_ref.t0), channel_id=1, source_target_pairs={{0,32},{8,40},{16,48},{24,56},{32,64},{40,72},{48,80},{56,88},{64,... | collective-permute-start | bytes 98312 | tf_op jit(solution)/shard_map/ppermute | solution.py:220
  34.7 2.4 %product.1 = (f32[1024,1024]{1,0:T(8,128)S(1)}, f32[1024,1024]{1,0:T(8,128)S(1)}, f32[1024,1024]{1,0:T(8,128)S(1)}, f32[1024,1024]{1,0:T(8,128)S(1)}, f32[128,1024]{1,0:T(8,128)S(1)}) custom-call(f32[8,1024]{1,0:T(8,128)S(1)} %get-tuple-element.56.stat_ref.t0, bf16[512,128]{1,0:T(8,128)(2,1)S(1)} %get-tuple-element.46.p0, ...), custom_call_target="tpu_custom_call" | custom-call | flops 1073741824 | bytes 1048576 | tf_op jit(solution)/shard_map/product/pallas_call | solution.py:236
  37.1 0.0 collective-permute-done.11.t3
  37.1 1.6 %collective-permute-done.10.t2 = f32[8,1024]{1,0:T(8,128)S(1)} collective-permute-done((f32[8,1024]{1,0:T(8,128)S(1)}, f32[8,1024]{1,0:T(8,128)S(1)}, u32[]{:S(2)}, u32[]{:S(2)}) %collective-permute-start.10) | collective-permute-done | bytes 32800 | tf_op jit(solution)/shard_map/ppermute | solution.py:220
  38.7 0.4 collective-permute-done.9.t1
  39.1 0.9 %remote.1 = (f32[4,1024]{1,0:T(4,128)S(1)}, f32[4,1024]{1,0:T(4,128)S(1)}, bf16[128,1024]{1,0:T(8,128)(2,1)S(1)}, bf16[1024,1024]{1,0:T(8,128)(2,1)S(1)}) custom-call(f32[8,1024]{1,0:T(8,128)S(1)} %get-tuple-element.56.stat_ref.t0, f32[8,1024]{1,0:T(8,128)S(1)} %collective-permute-done.9.t1, f32[8,1024]{1,0:T(8,128)S(1)} %collective-permute-done.10.t2, ...), custom_call_target="tpu_custom_call" | custom-call | flops 268435456 | bytes 1048576 | tf_op jit(solution)/shard_map/remote/pallas_call | solution.py:236
  40.0 1.7 %collective-permute-start.14 = (bf16[128,1024]{1,0:T(8,128)(2,1)S(1)}, bf16[128,1024]{1,0:T(8,128)(2,1)S(1)}, u32[]{:S(2)}, u32[]{:S(2)}) collective-permute-start(bf16[128,1024]{1,0:T(8,128)(2,1)S(1)} %get-tuple-element.73), channel_id=1, source_target_pairs={{0,64},{8,72},{16,80},{24,88},{32,96},{40,104},{48,112},{56,120},{... | collective-permute-start | bytes 786440 | tf_op jit(solution)/shard_map/ppermute | solution.py:220
  41.7 7.0 %local.1 = (bf16[128,1024]{1,0:T(8,128)(2,1)S(1)}, bf16[128,1024]{1,0:T(8,128)(2,1)S(1)}, bf16[128,1024]{1,0:T(8,128)(2,1)S(1)}, bf16[128,128]{1,0:T(8,128)(2,1)...) custom-call(f32[4,1024]{1,0:T(4,128)S(1)} %get-tuple-element.60.fact, ...), custom_call_target="tpu_custom_call" | custom-call | flops 2952790016 | bytes 1048576 | tf_op jit(solution)/shard_map/local/pallas_call | solution.py:236
  48.8 1.1 %collective-permute-start.12 = (bf16[128,1024]{1,0:T(8,128)(2,1)S(1)}, bf16[128,1024]{1,0:T(8,128)(2,1)S(1)}, u32[]{:S(2)}, u32[]{:S(2)}) collective-permute-start(bf16[128,1024]{1,0:T(8,128)(2,1)S(1)} %get-tuple-element.71), channel_id=1, source_target_pairs={{0,96},{8,104},{16,112},{24,120},{32,0},{40,8},{48,16},{56,24},{64... | collective-permute-start | bytes 786440 | tf_op jit(solution)/shard_map/ppermute | solution.py:220
  49.9 0.9 %collective-permute-start.13 = (bf16[128,1024]{1,0:T(8,128)(2,1)S(1)}, bf16[128,1024]{1,0:T(8,128)(2,1)S(1)}, u32[]{:S(2)}, u32[]{:S(2)}) collective-permute-start(bf16[128,1024]{1,0:T(8,128)(2,1)S(1)} %get-tuple-element.72), channel_id=1, source_target_pairs={{0,32},{8,40},{16,48},{24,56},{32,64},{40,72},{48,80},{56,88},{64,... | collective-permute-start | bytes 786440 | tf_op jit(solution)/shard_map/ppermute | solution.py:220
  50.8 2.7 %collective-permute-start.15 = (bf16[512,128]{1,0:T(8,128)(2,1)S(1)}, bf16[512,128]{1,0:T(8,128)(2,1)S(1)}, u32[]{:S(2)}, u32[]{:S(2)}) collective-permute-start(bf16[512,128]{1,0:T(8,128)(2,1)S(1)} %get-tuple-element.75), channel_id=1, source_target_pairs={{0,24},{8,0},{16,8},{24,16},{32,56},{40,32},{48,40},{56,48},{64,88... | collective-permute-start | bytes 393224 | tf_op jit(solution)/shard_map/ppermute | solution.py:220
  53.5 0.0 collective-permute-start.16
  53.5 0.0 collective-permute-done.14
  53.5 0.6 collective-permute-start.17
  54.1 1.1 %collective-permute-done.12 = bf16[128,1024]{1,0:T(8,128)(2,1)S(1)} collective-permute-done((bf16[128,1024]{1,0:T(8,128)(2,1)S(1)}, bf16[128,1024]{1,0:T(8,128)(2,1)S(1)}, u32[]{:S(2)}, u32[]{:S(2)}) %collective-permute-start.12) | collective-permute-done | bytes 262176 | tf_op jit(solution)/shard_map/ppermute | solution.py:220
  55.1 2.4 %collective-permute-done.13 = bf16[128,1024]{1,0:T(8,128)(2,1)S(1)} collective-permute-done((bf16[128,1024]{1,0:T(8,128)(2,1)S(1)}, bf16[128,1024]{1,0:T(8,128)(2,1)S(1)}, u32[]{:S(2)}, u32[]{:S(2)}) %collective-permute-start.13) | collective-permute-done | bytes 262176 | tf_op jit(solution)/shard_map/ppermute | solution.py:220
  57.5 0.9 %add_convert_fusion = bf16[128,1024]{1,0:T(8,128)(2,1)} fusion(bf16[128,1024]{1,0:T(8,128)(2,1)S(1)} %collective-permute-done.14, bf16[128,1024]{1,0:T(8,128)(2,1)S(1)} %collective-permute-done.13, bf16[128,1024]{1,0:T(8,128)(2,1)S(1)} %collective-permute-done.12, bf16[128,1024]{1,0:T(8,128)(2,1)S(1)} %get-tuple-element.70), kind=kLoop, calls=%fused_computation | loop fusion | flops 1048576 | bytes 1310720 | tf_op jit(solution)/shard_map/convert_element_type | solution.py:227
  58.4 0.0 collective-permute-done.15
  58.4 2.0 %collective-permute-done.16 = bf16[512,128]{1,0:T(8,128)(2,1)S(1)} collective-permute-done((bf16[512,128]{1,0:T(8,128)(2,1)S(1)}, bf16[512,128]{1,0:T(8,128)(2,1)S(1)}, u32[]{:S(2)}, u32[]{:S(2)}) %collective-permute-start.16) | collective-permute-done | bytes 131104 | tf_op jit(solution)/shard_map/ppermute | solution.py:220
  60.4 1.8 %collective-permute-done.17 = bf16[512,128]{1,0:T(8,128)(2,1)S(1)} collective-permute-done((bf16[512,128]{1,0:T(8,128)(2,1)S(1)}, bf16[512,128]{1,0:T(8,128)(2,1)S(1)}, u32[]{:S(2)}, u32[]{:S(2)}) %collective-permute-start.17) | collective-permute-done | bytes 131104 | tf_op jit(solution)/shard_map/ppermute | solution.py:220
  62.2 0.1 add_convert_fusion.1
  62.2 0.7 %fusion = (bf16[256,128]{1,0:T(8,128)(2,1)}, bf16[256,128]{1,0:T(8,128)(2,1)}) fusion(bf16[512,128]{1,0:T(8,128)(2,1)S(1)} %add_convert_fusion.1), kind=kLoop, calls=%fused_computation.2 | loop fusion | bytes 262144 | tf_op jit(solution)/shard_map/slice | solution.py:304
Async XLA Ops:
  0.6 9.6 %collective-permute-start.3 = (bf16[128,1024]{1,0:T(8,128)(2,1)}, bf16[128,1024]{1,0:T(8,128)(2,1)S(1)}, u32[]{:S(2)}, u32[]{:S(2)}) collective-permute-start(bf16[128,1024]{1,0:T(8,128)(2,1)} %q_hbm.1), channel_id=1, source_target_pairs={{0,32},{8,40},{16,48},{24,56},{32,64},{40,72},{48,80},{56,88},{64,... | collective-permute-start | bytes 786440 | tf_op jit(solution)/shard_map/ppermute | solution.py:220
  4.1 15.6 %collective-permute-start.7 = (bf16[128,1024]{1,0:T(8,128)(2,1)S(1)}, bf16[128,1024]{1,0:T(8,128)(2,1)S(1)}, u32[]{:S(2)}, u32[]{:S(2)}) collective-permute-start(bf16[128,1024]{1,0:T(8,128)(2,1)S(1)} %get-tuple-element.55.m0), channel_id=1, source_target_pairs={{0,96},{8,104},{16,112},{24,120},{32,0},{40,8},{48,16},{56,24},{64... | collective-permute-start | bytes 786440 | tf_op jit(solution)/shard_map/ppermute | solution.py:220
  5.8 9.3 %collective-permute-start = (bf16[512,128]{1,0:T(8,128)(2,1)S(1)}, bf16[512,128]{1,0:T(8,128)(2,1)S(1)}, u32[]{:S(2)}, u32[]{:S(2)}) collective-permute-start(bf16[512,128]{1,0:T(8,128)(2,1)S(1)} %get-tuple-element.46.p0), channel_id=1, source_target_pairs={{0,8},{8,16},{16,24},{24,0},{32,40},{40,48},{48,56},{56,32},{64,72... | collective-permute-start | bytes 393224 | tf_op jit(solution)/shard_map/ppermute | solution.py:220
  7.8 16.4 %collective-permute-start.5 = (bf16[128,1024]{1,0:T(8,128)(2,1)}, bf16[128,1024]{1,0:T(8,128)(2,1)S(1)}, u32[]{:S(2)}, u32[]{:S(2)}) collective-permute-start(bf16[128,1024]{1,0:T(8,128)(2,1)} %q_hbm.1), channel_id=1, source_target_pairs={{0,96},{8,104},{16,112},{24,120},{32,0},{40,8},{48,16},{56,24},{64... | collective-permute-start | bytes 786440 | tf_op jit(solution)/shard_map/ppermute | solution.py:220
  10.2 14.0 %collective-permute-start.4 = (bf16[128,1024]{1,0:T(8,128)(2,1)S(1)}, bf16[128,1024]{1,0:T(8,128)(2,1)S(1)}, u32[]{:S(2)}, u32[]{:S(2)}) collective-permute-start(bf16[128,1024]{1,0:T(8,128)(2,1)S(1)} %collective-permute-done.3.q1), channel_id=1, source_target_pairs={{0,32},{8,40},{16,48},{24,56},{32,64},{40,72},{48,80},{56,88},{64,... | collective-permute-start | bytes 786440 | tf_op jit(solution)/shard_map/ppermute | solution.py:220
  10.5 7.7 %collective-permute-start.2 = (bf16[512,128]{1,0:T(8,128)(2,1)S(1)}, bf16[512,128]{1,0:T(8,128)(2,1)S(1)}, u32[]{:S(2)}, u32[]{:S(2)}) collective-permute-start(bf16[512,128]{1,0:T(8,128)(2,1)S(1)} %get-tuple-element.46.p0), channel_id=1, source_target_pairs={{0,24},{8,0},{16,8},{24,16},{32,56},{40,32},{48,40},{56,48},{64,88... | collective-permute-start | bytes 393224 | tf_op jit(solution)/shard_map/ppermute | solution.py:220
  15.2 6.8 %collective-permute-start.1 = (bf16[512,128]{1,0:T(8,128)(2,1)S(1)}, bf16[512,128]{1,0:T(8,128)(2,1)S(1)}, u32[]{:S(2)}, u32[]{:S(2)}) collective-permute-start(bf16[512,128]{1,0:T(8,128)(2,1)S(1)} %collective-permute-done.p1), channel_id=1, source_target_pairs={{0,8},{8,16},{16,24},{24,0},{32,40},{40,48},{48,56},{56,32},{64,72... | collective-permute-start | bytes 393224 | tf_op jit(solution)/shard_map/ppermute | solution.py:220
  18.2 11.7 %collective-permute-start.6 = (bf16[128,1024]{1,0:T(8,128)(2,1)S(1)}, bf16[128,1024]{1,0:T(8,128)(2,1)S(1)}, u32[]{:S(2)}, u32[]{:S(2)}) collective-permute-start(bf16[128,1024]{1,0:T(8,128)(2,1)S(1)} %get-tuple-element.55.m0), channel_id=1, source_target_pairs={{0,32},{8,40},{16,48},{24,56},{32,64},{40,72},{48,80},{56,88},{64,... | collective-permute-start | bytes 786440 | tf_op jit(solution)/shard_map/ppermute | solution.py:220
  19.8 10.2 %collective-permute-start.8 = (bf16[128,1024]{1,0:T(8,128)(2,1)S(1)}, bf16[128,1024]{1,0:T(8,128)(2,1)S(1)}, u32[]{:S(2)}, u32[]{:S(2)}) collective-permute-start(bf16[128,1024]{1,0:T(8,128)(2,1)S(1)} %collective-permute-done.7.m3), channel_id=1, source_target_pairs={{0,96},{8,104},{16,112},{24,120},{32,0},{40,8},{48,16},{56,24},{64... | collective-permute-start | bytes 786440 | tf_op jit(solution)/shard_map/ppermute | solution.py:220
  30.3 6.8 %collective-permute-start.11 = (f32[8,1024]{1,0:T(8,128)S(1)}, f32[8,1024]{1,0:T(8,128)S(1)}, u32[]{:S(2)}, u32[]{:S(2)}) collective-permute-start(f32[8,1024]{1,0:T(8,128)S(1)} %get-tuple-element.56.stat_ref.t0), channel_id=1, source_target_pairs={{0,96},{8,104},{16,112},{24,120},{32,0},{40,8},{48,16},{56,24},{64... | collective-permute-start | bytes 98312 | tf_op jit(solution)/shard_map/ppermute | solution.py:220
  33.3 5.4 %collective-permute-start.10 = (f32[8,1024]{1,0:T(8,128)S(1)}, f32[8,1024]{1,0:T(8,128)S(1)}, u32[]{:S(2)}, u32[]{:S(2)}) collective-permute-start(f32[8,1024]{1,0:T(8,128)S(1)} %get-tuple-element.56.stat_ref.t0), channel_id=1, source_target_pairs={{0,64},{8,72},{16,80},{24,88},{32,96},{40,104},{48,112},{56,120},{... | collective-permute-start | bytes 98312 | tf_op jit(solution)/shard_map/ppermute | solution.py:220
  34.0 5.1 %collective-permute-start.9 = (f32[8,1024]{1,0:T(8,128)S(1)}, f32[8,1024]{1,0:T(8,128)S(1)}, u32[]{:S(2)}, u32[]{:S(2)}) collective-permute-start(f32[8,1024]{1,0:T(8,128)S(1)} %get-tuple-element.56.stat_ref.t0), channel_id=1, source_target_pairs={{0,32},{8,40},{16,48},{24,56},{32,64},{40,72},{48,80},{56,88},{64,... | collective-permute-start | bytes 98312 | tf_op jit(solution)/shard_map/ppermute | solution.py:220
  40.0 13.5 %collective-permute-start.14 = (bf16[128,1024]{1,0:T(8,128)(2,1)S(1)}, bf16[128,1024]{1,0:T(8,128)(2,1)S(1)}, u32[]{:S(2)}, u32[]{:S(2)}) collective-permute-start(bf16[128,1024]{1,0:T(8,128)(2,1)S(1)} %get-tuple-element.73), channel_id=1, source_target_pairs={{0,64},{8,72},{16,80},{24,88},{32,96},{40,104},{48,112},{56,120},{... | collective-permute-start | bytes 786440 | tf_op jit(solution)/shard_map/ppermute | solution.py:220
  48.8 6.4 %collective-permute-start.12 = (bf16[128,1024]{1,0:T(8,128)(2,1)S(1)}, bf16[128,1024]{1,0:T(8,128)(2,1)S(1)}, u32[]{:S(2)}, u32[]{:S(2)}) collective-permute-start(bf16[128,1024]{1,0:T(8,128)(2,1)S(1)} %get-tuple-element.71), channel_id=1, source_target_pairs={{0,96},{8,104},{16,112},{24,120},{32,0},{40,8},{48,16},{56,24},{64... | collective-permute-start | bytes 786440 | tf_op jit(solution)/shard_map/ppermute | solution.py:220
  49.9 7.6 %collective-permute-start.13 = (bf16[128,1024]{1,0:T(8,128)(2,1)S(1)}, bf16[128,1024]{1,0:T(8,128)(2,1)S(1)}, u32[]{:S(2)}, u32[]{:S(2)}) collective-permute-start(bf16[128,1024]{1,0:T(8,128)(2,1)S(1)} %get-tuple-element.72), channel_id=1, source_target_pairs={{0,32},{8,40},{16,48},{24,56},{32,64},{40,72},{48,80},{56,88},{64,... | collective-permute-start | bytes 786440 | tf_op jit(solution)/shard_map/ppermute | solution.py:220
  50.8 7.6 %collective-permute-start.15 = (bf16[512,128]{1,0:T(8,128)(2,1)S(1)}, bf16[512,128]{1,0:T(8,128)(2,1)S(1)}, u32[]{:S(2)}, u32[]{:S(2)}) collective-permute-start(bf16[512,128]{1,0:T(8,128)(2,1)S(1)} %get-tuple-element.75), channel_id=1, source_target_pairs={{0,24},{8,0},{16,8},{24,16},{32,56},{40,32},{48,40},{56,48},{64,88... | collective-permute-start | bytes 393224 | tf_op jit(solution)/shard_map/ppermute | solution.py:220
  53.5 6.9 %collective-permute-start.16 = (bf16[512,128]{1,0:T(8,128)(2,1)S(1)}, bf16[512,128]{1,0:T(8,128)(2,1)S(1)}, u32[]{:S(2)}, u32[]{:S(2)}) collective-permute-start(bf16[512,128]{1,0:T(8,128)(2,1)S(1)} %get-tuple-element.76), channel_id=1, source_target_pairs={{0,8},{8,16},{16,24},{24,0},{32,40},{40,48},{48,56},{56,32},{64,72... | collective-permute-start | bytes 393224 | tf_op jit(solution)/shard_map/ppermute | solution.py:220
  53.5 8.7 %collective-permute-start.17 = (bf16[512,128]{1,0:T(8,128)(2,1)S(1)}, bf16[512,128]{1,0:T(8,128)(2,1)S(1)}, u32[]{:S(2)}, u32[]{:S(2)}) collective-permute-start(bf16[512,128]{1,0:T(8,128)(2,1)S(1)} %get-tuple-element.78), channel_id=1, source_target_pairs={{0,16},{8,24},{16,0},{24,8},{32,48},{40,56},{48,32},{56,40},{64,80... | collective-permute-start | bytes 393224 | tf_op jit(solution)/shard_map/ppermute | solution.py:220

commit v2 on v1

--- a/solution.py
+++ b/solution.py
@@ -78,11 +78,10 @@
     return jnp.sum(totals, 0, keepdims=True)
 
 
-def summary(highest, totals, attended, n, high_ref, lse_ref, a_ref):
+def summary(highest, totals, n, high_ref, lse_ref):
     high = highest * (HEAD_DIM**-0.5 * LOG2E)
     high_ref[n : n + 1, :] = high
     lse_ref[n : n + 1, :] = high + jnp.log2(totals)
-    a_ref[...] = attended / totals
 
 
 def own_kernel(q_ref, kr, vr, p0, p1, p2, p3, w_ref, high_ref, lse_ref, a_ref, s_ref):
@@ -97,31 +96,50 @@
     highest = score_block(s_ref, rows, plane_of(pieces, 0), q, highest)
     highest = jnp.max(highest, 0, keepdims=True)
     totals = weigh(s_ref, w_ref, highest)
-    attended = dot(vr[...], w_ref[0:rows, :], 0, 0) + dot(
+    summary(highest, totals, 0, high_ref, lse_ref)
+    a_ref[...] = dot(vr[...], w_ref[0:rows, :], 0, 0) + dot(
         plane_of(pieces, 1), w_ref[rows:, :], 0, 0
     )
-    summary(highest, totals, attended, 0, high_ref, lse_ref, a_ref)
 
 
 def other_kernel(q1, q2, q3, p0, p1, p2, p3, w1, w2, w3, high_ref, lse_ref, a1, a2, a3, s1, s2, s3):
     pieces = (p0, p1, p2, p3)
     keys, values = plane_of(pieces, 0), plane_of(pieces, 1)
-    for n, (q, w, a, s_ref) in enumerate(((q1, w1, a1, s1), (q2, w2, a2, s2), (q3, w3, a3, s3))):
-        highest = jnp.full((16, w.shape[1]), -jnp.inf, F32)
-        highest = score_block(s_ref, 0, keys, stack_heads(q), highest)
-        highest = jnp.max(highest, 0, keepdims=True)
-        totals = weigh(s_ref, w, highest)
-        summary(highest, totals, dot(values, w[...], 0, 0), n, high_ref, lse_ref, a)
+    plane, wide = w1.shape
+    group, step, small = 16, 256, 64
+    scale = HEAD_DIM**-0.5 * LOG2E
+    jobs = ((q1, w1, a1, s1), (q2, w2, a2, s2), (q3, w3, a3, s3))
+    before = None
+    for n in range(len(jobs) + 1):
+        if n < len(jobs):
+            q = stack_heads(jobs[n][0])
+            top = jnp.full((group, wide), -jnp.inf, F32)
+        totals = jnp.zeros((group, wide), F32)
+        for r in range(0, plane, step):
+            if n < len(jobs):
+                s = dot(keys[r : r + step, :], q, 1, 1)
+                jobs[n][3][r : r + step, :] = s
+                top = jnp.maximum(top, jnp.max(s.reshape(step // group, group, wide), 0))
+            if before is not None:
+                for t in range(r, r + step, small):
+                    w = jnp.exp2((jobs[n - 1][3][t : t + small, :] - before) * scale)
+                    jobs[n - 1][1][t : t + small, :] = w.astype(BF16)
+                    totals = totals + jnp.sum(w.reshape(small // group, group, wide), 0)
+        if before is not None:
+            summary(before, jnp.sum(totals, 0, keepdims=True), n - 1, high_ref, lse_ref)
+            jobs[n - 1][2][...] = dot(values, jobs[n - 1][1][...], 0, 0)
+        if n < len(jobs):
+            before = jnp.max(top, 0, keepdims=True)
 
 
 def delta_kernel(high0, high123, lse0, lse123, a0, a1, a2, a3, m0, m1, m2, m3, high_ref, stat_ref):
     high_ref[0:1, :] = high0[...]
     high_ref[1:SIDE, :] = high123[...]
-    stat_ref[0:1, :] = lse0[...]
     for d, (a, m) in enumerate(zip((a0, a1, a2, a3), (m0, m1, m2, m3))):
-        if d:
-            stat_ref[2 * d : 2 * d + 1, :] = lse123[d - 1 : d, :]
+        lse = lse123[d - 1 : d, :] if d else lse0[...]
+        stat_ref[2 * d : 2 * d + 1, :] = lse
         part = jnp.sum(m[...].astype(F32) * a[...], 0, keepdims=True)
+        part = part * jnp.exp2(high_ref[d : d + 1, :] - lse)
         stat_ref[2 * d + 1 : 2 * d + 2, :] = part
 
 
@@ -183,14 +201,25 @@
     def masked(m, d):
         return (m[...].astype(F32) * factor_ref[d : d + 1, :]).astype(BF16)
 
-    keys = dot(ds2[...], stack_heads(q2), 1, 0)
-    values = dot(w2[...], masked(m2, 2), 1, 1)
+    plane = w1.shape[0]
+    step = 512
+    starts = range(0, plane, step)
+    q, g = stack_heads(q2), masked(m2, 2)
+    keys = [dot(ds2[r : r + step, :], q, 1, 0) for r in starts]
+    values = [dot(w2[r : r + step, :], g, 1, 1) for r in starts]
     for d, q, m, w, x, out in ((1, q1, m1, w1, x1, dq1), (3, q3, m3, w3, x3, dq3)):
         factor, delta = pair(d)
-        ds = w[...] * ((x[...] - delta) * factor).astype(BF16)
-        turn_back(dot(plane_keys, ds, 0, 0), out)
-        keys = keys + dot(ds, stack_heads(q), 1, 0)
-        values = values + dot(w[...], masked(m, d), 1, 1)
+        q, g = stack_heads(q), masked(m, d)
+        grad = None
+        for n, r in enumerate(starts):
+            rows_r = slice(r, r + step)
+            ds = w[rows_r, :] * ((x[rows_r, :] - delta) * factor).astype(BF16)
+            values[n] = values[n] + dot(w[rows_r, :], g, 1, 1)
+            keys[n] = keys[n] + dot(ds, q, 1, 0)
+            part = dot(plane_keys[rows_r, :], ds, 0, 0)
+            grad = part if grad is None else grad + part
+        turn_back(grad, out)
+    keys, values = jnp.concatenate(keys, 0), jnp.concatenate(values, 0)
     factor, delta = pair(0)
     q = stack_heads(q0)
     g = masked(m0, 0)
@@ -270,7 +299,7 @@
         [pltpu.VMEM((rows, cols), BF16), pltpu.SMEM((1,), jnp.int32),
          pltpu.SemaphoreType.DMA((7,))], space=pltpu.HBM)
     p1, p3 = (send(piece, shift_z(d)) for d in (1, 3))
-    pieces = (piece, p1, send(p1, shift_z(1)), p3)
+    pieces = (piece, p1, send(p3, shift_z(3)), p3)
     m1, m3 = (send(m0, shift_y(d)) for d in (1, 3))
     m2 = send(m3, shift_y(3))
     w0, high0, lse0, a0 = call(
@@ -297,7 +326,7 @@
         local_kernel, "local", [flat] * 3 + [small, small] + [both] * 4,
         (factors, delta, *pieces, kr, w0, w1, w2, w3, x0, x1, x3, xr, ds2,
          m0, m1, m2, m3, q0, q1, q2, q3), 16, flops=11 * unit)
-    o2, unused = lax.optimization_barrier((o2, back2))
+    dq1, unused = lax.optimization_barrier((dq1, back2))
     total = combine(o0, [send(x, shift_z(-d)) for d, x in ((1, o1), (3, o3), (2, o2))])
     returned = [send(x, shift_y(-d)) for d, x in ((1, dq1), (3, dq3))] + [back2]
     grad_queries = combine(dq0, returned)

time: 63 us -> 60.8 us (0.965)
  waiting for transfers between devices: 13.5 us -> 10.1 us
  starting transfers between devices: 26.6 us -> 28.4 us
  Pallas kernels: 19.8 us -> 18.7 us
    ppermute x18, waiting for transfers between devices: 13.5 us -> 10.1 us  [send(): return lax.ppermute(x, 'resp', perm)]
    ppermute x18, starting transfers between devices: 26.6 us -> 28.4 us  [send(): return lax.ppermute(x, 'resp', perm)]
    pallas_call x7, Pallas kernels: 19.8 us -> 18.7 us  [call(): pl.pallas_call(kernel, out_shape=[jax.ShapeDtypeStruct(*o) for o in outs]...]
  transfers between devices with their start and end apart: 18 -> 18, of which waited for: 9 -> 5; matrix products, arithmetic and copies ran while one was open for 1% -> 1% of each run, Pallas kernels for 29% -> 29%
where the time goes in v2:
time: 60.8 us; the launch traced here: 60.1 us
  starting transfers between devices  28.4 us (47%)
  Pallas kernels  18.7 us (31%)
  waiting for transfers between devices  10.1 us (17%)
  between operations  1.38 us (2%)
  other arithmetic  0.95 us (2%)
  local copies, waits for them, and re-layouts  0.66 us (1%)
    ppermute x18, starting transfers between devices, send(): return lax.ppermute(x, 'resp', perm)  28.4 us
    pallas_call x7, Pallas kernels, call(): pl.pallas_call(kernel, out_shape=[jax.ShapeDtypeStruct(*o) for o in outs]...  18.7 us
    ppermute x18, waiting for transfers between devices, send(): return lax.ppermute(x, 'resp', perm)  10.1 us
  transfers between devices with their start and end apart: 18, of which 5 were waited for; matrix products, arithmetic and copies ran while one was open for 1% of the time, Pallas kernels for 29%

profile of v2, /device:TPU:2, one launch (start us, length us, event | category | flops | bytes accessed | tf_op | source)
XLA Modules:
  0.0 60.1 jit_solution(11933298412522553834)
XLA Ops:
  0.6 1.7 %collective-permute-start.3 = (bf16[128,1024]{1,0:T(8,128)(2,1)}, bf16[128,1024]{1,0:T(8,128)(2,1)S(1)}, u32[]{:S(2)}, u32[]{:S(2)}) collective-permute-start(bf16[128,1024]{1,0:T(8,128)(2,1)} %q_hbm.1), channel_id=1, source_target_pairs={{0,32},{8,40},{16,48},{24,56},{32,64},{40,72},{48,80},{56,88},{64,... | collective-permute-start | bytes 786440 | tf_op jit(solution)/shard_map/ppermute | solution.py:249
  2.9 1.2 %prepare.1 = (bf16[128,1024]{1,0:T(8,128)(2,1)S(1)}, bf16[128,1024]{1,0:T(8,128)(2,1)S(1)}, bf16[512,128]{1,0:T(8,128)(2,1)S(1)}, bf16[128,128]{1,0:T(8,128)(2,1)S(1)}, bf16[128,128]{1,0:T(8,128)(2,1)S(1)}) custom-call(s32[1]{0:T(128)S(6)} %copy.12.len_hbm, bf16[128,1024]{1,0:T(8,128)(2,1)} %q_hbm.1, bf16[128,1024]{1,0:T(8,128)(2,1)} %g_hbm.1, ...), custom_call_target="tpu_custom_call" | custom-call | bytes 1048576 | tf_op jit(solution)/shard_map/prepare/pallas_call | solution.py:265
  4.1 1.7 %collective-permute-start.7 = (bf16[128,1024]{1,0:T(8,128)(2,1)S(1)}, bf16[128,1024]{1,0:T(8,128)(2,1)S(1)}, u32[]{:S(2)}, u32[]{:S(2)}) collective-permute-start(bf16[128,1024]{1,0:T(8,128)(2,1)S(1)} %get-tuple-element.55.m0), channel_id=1, source_target_pairs={{0,96},{8,104},{16,112},{24,120},{32,0},{40,8},{48,16},{56,24},{64... | collective-permute-start | bytes 786440 | tf_op jit(solution)/shard_map/ppermute | solution.py:249
  5.8 4.6 %collective-permute-start.1 = (bf16[512,128]{1,0:T(8,128)(2,1)S(1)}, bf16[512,128]{1,0:T(8,128)(2,1)S(1)}, u32[]{:S(2)}, u32[]{:S(2)}) collective-permute-start(bf16[512,128]{1,0:T(8,128)(2,1)S(1)} %get-tuple-element.46.p0), channel_id=1, source_target_pairs={{0,24},{8,0},{16,8},{24,16},{32,56},{40,32},{48,40},{56,48},{64,88... | collective-permute-start | bytes 393224 | tf_op jit(solution)/shard_map/ppermute | solution.py:249
  10.5 1.8 %collective-permute-start.5 = (bf16[128,1024]{1,0:T(8,128)(2,1)}, bf16[128,1024]{1,0:T(8,128)(2,1)S(1)}, u32[]{:S(2)}, u32[]{:S(2)}) collective-permute-start(bf16[128,1024]{1,0:T(8,128)(2,1)} %q_hbm.1), channel_id=1, source_target_pairs={{0,96},{8,104},{16,112},{24,120},{32,0},{40,8},{48,16},{56,24},{64... | collective-permute-start | bytes 786440 | tf_op jit(solution)/shard_map/ppermute | solution.py:249
  12.3 0.0 collective-permute-done.3.q1
  12.3 0.2 collective-permute-start.4
  12.5 0.0 collective-permute-start
  12.5 1.7 %collective-permute-done.1.p3 = bf16[512,128]{1,0:T(8,128)(2,1)S(1)} collective-permute-done((bf16[512,128]{1,0:T(8,128)(2,1)S(1)}, bf16[512,128]{1,0:T(8,128)(2,1)S(1)}, u32[]{:S(2)}, u32[]{:S(2)}) %collective-permute-start.1) | collective-permute-done | bytes 131104 | tf_op jit(solution)/shard_map/ppermute | solution.py:249
  14.2 4.4 %collective-permute-start.2 = (bf16[512,128]{1,0:T(8,128)(2,1)S(1)}, bf16[512,128]{1,0:T(8,128)(2,1)S(1)}, u32[]{:S(2)}, u32[]{:S(2)}) collective-permute-start(bf16[512,128]{1,0:T(8,128)(2,1)S(1)} %collective-permute-done.1.p3), channel_id=1, source_target_pairs={{0,24},{8,0},{16,8},{24,16},{32,56},{40,32},{48,40},{56,48},{64,88... | collective-permute-start | bytes 393224 | tf_op jit(solution)/shard_map/ppermute | solution.py:249
  18.6 1.2 %collective-permute-done.p1 = bf16[512,128]{1,0:T(8,128)(2,1)S(1)} collective-permute-done((bf16[512,128]{1,0:T(8,128)(2,1)S(1)}, bf16[512,128]{1,0:T(8,128)(2,1)S(1)}, u32[]{:S(2)}, u32[]{:S(2)}) %collective-permute-start) | collective-permute-done | bytes 131104 | tf_op jit(solution)/shard_map/ppermute | solution.py:249
  19.8 0.8 %collective-permute-start.6 = (bf16[128,1024]{1,0:T(8,128)(2,1)S(1)}, bf16[128,1024]{1,0:T(8,128)(2,1)S(1)}, u32[]{:S(2)}, u32[]{:S(2)}) collective-permute-start(bf16[128,1024]{1,0:T(8,128)(2,1)S(1)} %get-tuple-element.55.m0), channel_id=1, source_target_pairs={{0,32},{8,40},{16,48},{24,56},{32,64},{40,72},{48,80},{56,88},{64,... | collective-permute-start | bytes 786440 | tf_op jit(solution)/shard_map/ppermute | solution.py:249
  20.6 0.0 collective-permute-done.7.m3
  20.6 2.4 %collective-permute-start.8 = (bf16[128,1024]{1,0:T(8,128)(2,1)S(1)}, bf16[128,1024]{1,0:T(8,128)(2,1)S(1)}, u32[]{:S(2)}, u32[]{:S(2)}) collective-permute-start(bf16[128,1024]{1,0:T(8,128)(2,1)S(1)} %collective-permute-done.7.m3), channel_id=1, source_target_pairs={{0,96},{8,104},{16,112},{24,120},{32,0},{40,8},{48,16},{56,24},{64... | collective-permute-start | bytes 786440 | tf_op jit(solution)/shard_map/ppermute | solution.py:249
  23.0 0.0 collective-permute-done.2.p2
  23.1 2.3 %own.1 = (bf16[1152,1024]{1,0:T(8,128)(2,1)S(1)}, f32[1,1024]{1,0:T(1,128)S(1)}, f32[1,1024]{1,0:T(1,128)S(1)}, f32[128,1024]{1,0:T(8,128)S(1)}) custom-call(bf16[128,1024]{1,0:T(8,128)(2,1)S(1)} %get-tuple-element.43.q_ref.q0, bf16[128,128]{1,0:T(8,128)(2,1)S(1)} %get-tuple-element.44.kr, bf16[128,128]{1,0:T(8,128)(2,1)S(1)} %get-tuple-element.45.vr, ...), custom_call_target="tpu_custom_call" | custom-call | flops 536870912 | bytes 1048576 | tf_op jit(solution)/shard_map/own/pallas_call | solution.py:265
  25.3 0.0 collective-permute-done.5.q3
  25.3 0.0 collective-permute-done.4.q2
  25.3 5.2 %other.1 = (bf16[1024,1024]{1,0:T(8,128)(2,1)S(1)}, bf16[1024,1024]{1,0:T(8,128)(2,1)S(1)}, bf16[1024,1024]{1,0:T(8,128)(2,1)S(1)}, f32[3,1024]{1,0:T(4,128)S(1)...) custom-call(bf16[128,1024]{1,0:T(8,128)(2,1)S(1)} %collective-permute-don, ...), custom_call_target="tpu_custom_call" | custom-call | flops 1610612736 | bytes 1048576 | tf_op jit(solution)/shard_map/other/pallas_call | solution.py:265
  30.5 0.0 collective-permute-done.6.m1
  30.5 0.0 collective-permute-done.8.m2
  30.5 0.4 delta.1
  30.9 1.8 %collective-permute-start.11 = (f32[8,1024]{1,0:T(8,128)S(1)}, f32[8,1024]{1,0:T(8,128)S(1)}, u32[]{:S(2)}, u32[]{:S(2)}) collective-permute-start(f32[8,1024]{1,0:T(8,128)S(1)} %get-tuple-element.56.stat_ref.t0), channel_id=1, source_target_pairs={{0,96},{8,104},{16,112},{24,120},{32,0},{40,8},{48,16},{56,24},{64... | collective-permute-start | bytes 98312 | tf_op jit(solution)/shard_map/ppermute | solution.py:249
  32.7 0.0 collective-permute-start.10
  32.7 1.0 %collective-permute-start.9 = (f32[8,1024]{1,0:T(8,128)S(1)}, f32[8,1024]{1,0:T(8,128)S(1)}, u32[]{:S(2)}, u32[]{:S(2)}) collective-permute-start(f32[8,1024]{1,0:T(8,128)S(1)} %get-tuple-element.56.stat_ref.t0), channel_id=1, source_target_pairs={{0,32},{8,40},{16,48},{24,56},{32,64},{40,72},{48,80},{56,88},{64,... | collective-permute-start | bytes 98312 | tf_op jit(solution)/shard_map/ppermute | solution.py:249
  33.6 2.4 %product.1 = (f32[1024,1024]{1,0:T(8,128)S(1)}, f32[1024,1024]{1,0:T(8,128)S(1)}, f32[1024,1024]{1,0:T(8,128)S(1)}, f32[1024,1024]{1,0:T(8,128)S(1)}, f32[128,1024]{1,0:T(8,128)S(1)}) custom-call(f32[8,1024]{1,0:T(8,128)S(1)} %get-tuple-element.56.stat_ref.t0, bf16[512,128]{1,0:T(8,128)(2,1)S(1)} %get-tuple-element.46.p0, ...), custom_call_target="tpu_custom_call" | custom-call | flops 1073741824 | bytes 1048576 | tf_op jit(solution)/shard_map/product/pallas_call | solution.py:265
  36.0 0.0 collective-permute-done.11.t3
  36.0 2.1 %collective-permute-done.10.t2 = f32[8,1024]{1,0:T(8,128)S(1)} collective-permute-done((f32[8,1024]{1,0:T(8,128)S(1)}, f32[8,1024]{1,0:T(8,128)S(1)}, u32[]{:S(2)}, u32[]{:S(2)}) %collective-permute-start.10) | collective-permute-done | bytes 32800 | tf_op jit(solution)/shard_map/ppermute | solution.py:249
  38.1 0.0 collective-permute-done.9.t1
  38.2 0.9 %remote.1 = (f32[4,1024]{1,0:T(4,128)S(1)}, f32[4,1024]{1,0:T(4,128)S(1)}, bf16[128,1024]{1,0:T(8,128)(2,1)S(1)}, bf16[1024,1024]{1,0:T(8,128)(2,1)S(1)}) custom-call(f32[8,1024]{1,0:T(8,128)S(1)} %get-tuple-element.56.stat_ref.t0, f32[8,1024]{1,0:T(8,128)S(1)} %collective-permute-done.9.t1, f32[8,1024]{1,0:T(8,128)S(1)} %collective-permute-done.10.t2, ...), custom_call_target="tpu_custom_call" | custom-call | flops 268435456 | bytes 1048576 | tf_op jit(solution)/shard_map/remote/pallas_call | solution.py:265
  39.1 2.3 %collective-permute-start.12 = (bf16[128,1024]{1,0:T(8,128)(2,1)S(1)}, bf16[128,1024]{1,0:T(8,128)(2,1)S(1)}, u32[]{:S(2)}, u32[]{:S(2)}) collective-permute-start(bf16[128,1024]{1,0:T(8,128)(2,1)S(1)} %get-tuple-element.72), channel_id=1, source_target_pairs={{0,64},{8,72},{16,80},{24,88},{32,96},{40,104},{48,112},{56,120},{... | collective-permute-start | bytes 786440 | tf_op jit(solution)/shard_map/ppermute | solution.py:249
  41.4 6.4 %local.1 = (bf16[128,1024]{1,0:T(8,128)(2,1)S(1)}, bf16[128,1024]{1,0:T(8,128)(2,1)S(1)}, bf16[128,1024]{1,0:T(8,128)(2,1)S(1)}, bf16[128,128]{1,0:T(8,128)(2,1)...) custom-call(f32[4,1024]{1,0:T(4,128)S(1)} %get-tuple-element.60.fact, ...), custom_call_target="tpu_custom_call" | custom-call | flops 2952790016 | bytes 1048576 | tf_op jit(solution)/shard_map/local/pallas_call | solution.py:265
  47.8 1.8 %collective-permute-start.15 = (bf16[512,128]{1,0:T(8,128)(2,1)S(1)}, bf16[512,128]{1,0:T(8,128)(2,1)S(1)}, u32[]{:S(2)}, u32[]{:S(2)}) collective-permute-start(bf16[512,128]{1,0:T(8,128)(2,1)S(1)} %get-tuple-element.76), channel_id=1, source_target_pairs={{0,24},{8,0},{16,8},{24,16},{32,56},{40,32},{48,40},{56,48},{64,88... | collective-permute-start | bytes 393224 | tf_op jit(solution)/shard_map/ppermute | solution.py:249
  49.5 0.2 collective-permute-start.16
  49.8 0.4 collective-permute-start.17
  50.2 1.0 %collective-permute-start.14 = (bf16[128,1024]{1,0:T(8,128)(2,1)S(1)}, bf16[128,1024]{1,0:T(8,128)(2,1)S(1)}, u32[]{:S(2)}, u32[]{:S(2)}) collective-permute-start(bf16[128,1024]{1,0:T(8,128)(2,1)S(1)} %get-tuple-element.74), channel_id=1, source_target_pairs={{0,32},{8,40},{16,48},{24,56},{32,64},{40,72},{48,80},{56,88},{64,... | collective-permute-start | bytes 786440 | tf_op jit(solution)/shard_map/ppermute | solution.py:249
  51.2 0.0 collective-permute-done.12
  51.2 2.3 %collective-permute-start.13 = (bf16[128,1024]{1,0:T(8,128)(2,1)S(1)}, bf16[128,1024]{1,0:T(8,128)(2,1)S(1)}, u32[]{:S(2)}, u32[]{:S(2)}) collective-permute-start(bf16[128,1024]{1,0:T(8,128)(2,1)S(1)} %get-tuple-element.73), channel_id=1, source_target_pairs={{0,96},{8,104},{16,112},{24,120},{32,0},{40,8},{48,16},{56,24},{64... | collective-permute-start | bytes 786440 | tf_op jit(solution)/shard_map/ppermute | solution.py:249
  53.4 0.0 collective-permute-done.15
  53.4 3.0 %collective-permute-done.16 = bf16[512,128]{1,0:T(8,128)(2,1)S(1)} collective-permute-done((bf16[512,128]{1,0:T(8,128)(2,1)S(1)}, bf16[512,128]{1,0:T(8,128)(2,1)S(1)}, u32[]{:S(2)}, u32[]{:S(2)}) %collective-permute-start.16) | collective-permute-done | bytes 131104 | tf_op jit(solution)/shard_map/ppermute | solution.py:249
  56.4 2.0 %collective-permute-done.17 = bf16[512,128]{1,0:T(8,128)(2,1)S(1)} collective-permute-done((bf16[512,128]{1,0:T(8,128)(2,1)S(1)}, bf16[512,128]{1,0:T(8,128)(2,1)S(1)}, u32[]{:S(2)}, u32[]{:S(2)}) %collective-permute-start.17) | collective-permute-done | bytes 131104 | tf_op jit(solution)/shard_map/ppermute | solution.py:249
  58.5 0.1 add_convert_fusion.1
  58.5 0.7 %fusion = (bf16[256,128]{1,0:T(8,128)(2,1)}, bf16[256,128]{1,0:T(8,128)(2,1)}) fusion(bf16[512,128]{1,0:T(8,128)(2,1)S(1)} %add_convert_fusion.1), kind=kLoop, calls=%fused_computation.2 | loop fusion | bytes 262144 | tf_op jit(solution)/shard_map/slice | solution.py:333
  59.2 0.0 collective-permute-done.14
  59.2 0.0 collective-permute-done.13
  59.2 0.9 %add_convert_fusion = bf16[128,1024]{1,0:T(8,128)(2,1)} fusion(bf16[128,1024]{1,0:T(8,128)(2,1)S(1)} %collective-permute-done.12, bf16[128,1024]{1,0:T(8,128)(2,1)S(1)} %collective-permute-done.14, bf16[128,1024]{1,0:T(8,128)(2,1)S(1)} %collective-permute-done.13, bf16[128,1024]{1,0:T(8,128)(2,1)S(1)} %get-tuple-element.70), kind=kLoop, calls=%fused_computation | loop fusion | flops 1048576 | bytes 1310720 | tf_op jit(solution)/shard_map/convert_element_type | solution.py:256
Async XLA Ops:
  0.6 11.6 %collective-permute-start.3 = (bf16[128,1024]{1,0:T(8,128)(2,1)}, bf16[128,1024]{1,0:T(8,128)(2,1)S(1)}, u32[]{:S(2)}, u32[]{:S(2)}) collective-permute-start(bf16[128,1024]{1,0:T(8,128)(2,1)} %q_hbm.1), channel_id=1, source_target_pairs={{0,32},{8,40},{16,48},{24,56},{32,64},{40,72},{48,80},{56,88},{64,... | collective-permute-start | bytes 786440 | tf_op jit(solution)/shard_map/ppermute | solution.py:249
  4.1 16.5 %collective-permute-start.7 = (bf16[128,1024]{1,0:T(8,128)(2,1)S(1)}, bf16[128,1024]{1,0:T(8,128)(2,1)S(1)}, u32[]{:S(2)}, u32[]{:S(2)}) collective-permute-start(bf16[128,1024]{1,0:T(8,128)(2,1)S(1)} %get-tuple-element.55.m0), channel_id=1, source_target_pairs={{0,96},{8,104},{16,112},{24,120},{32,0},{40,8},{48,16},{56,24},{64... | collective-permute-start | bytes 786440 | tf_op jit(solution)/shard_map/ppermute | solution.py:249
  5.8 8.4 %collective-permute-start.1 = (bf16[512,128]{1,0:T(8,128)(2,1)S(1)}, bf16[512,128]{1,0:T(8,128)(2,1)S(1)}, u32[]{:S(2)}, u32[]{:S(2)}) collective-permute-start(bf16[512,128]{1,0:T(8,128)(2,1)S(1)} %get-tuple-element.46.p0), channel_id=1, source_target_pairs={{0,24},{8,0},{16,8},{24,16},{32,56},{40,32},{48,40},{56,48},{64,88... | collective-permute-start | bytes 393224 | tf_op jit(solution)/shard_map/ppermute | solution.py:249
  10.5 14.8 %collective-permute-start.5 = (bf16[128,1024]{1,0:T(8,128)(2,1)}, bf16[128,1024]{1,0:T(8,128)(2,1)S(1)}, u32[]{:S(2)}, u32[]{:S(2)}) collective-permute-start(bf16[128,1024]{1,0:T(8,128)(2,1)} %q_hbm.1), channel_id=1, source_target_pairs={{0,96},{8,104},{16,112},{24,120},{32,0},{40,8},{48,16},{56,24},{64... | collective-permute-start | bytes 786440 | tf_op jit(solution)/shard_map/ppermute | solution.py:249
  12.3 13.1 %collective-permute-start.4 = (bf16[128,1024]{1,0:T(8,128)(2,1)S(1)}, bf16[128,1024]{1,0:T(8,128)(2,1)S(1)}, u32[]{:S(2)}, u32[]{:S(2)}) collective-permute-start(bf16[128,1024]{1,0:T(8,128)(2,1)S(1)} %collective-permute-done.3.q1), channel_id=1, source_target_pairs={{0,32},{8,40},{16,48},{24,56},{32,64},{40,72},{48,80},{56,88},{64,... | collective-permute-start | bytes 786440 | tf_op jit(solution)/shard_map/ppermute | solution.py:249
  12.5 7.3 %collective-permute-start = (bf16[512,128]{1,0:T(8,128)(2,1)S(1)}, bf16[512,128]{1,0:T(8,128)(2,1)S(1)}, u32[]{:S(2)}, u32[]{:S(2)}) collective-permute-start(bf16[512,128]{1,0:T(8,128)(2,1)S(1)} %get-tuple-element.46.p0), channel_id=1, source_target_pairs={{0,8},{8,16},{16,24},{24,0},{32,40},{40,48},{48,56},{56,32},{64,72... | collective-permute-start | bytes 393224 | tf_op jit(solution)/shard_map/ppermute | solution.py:249
  14.2 8.8 %collective-permute-start.2 = (bf16[512,128]{1,0:T(8,128)(2,1)S(1)}, bf16[512,128]{1,0:T(8,128)(2,1)S(1)}, u32[]{:S(2)}, u32[]{:S(2)}) collective-permute-start(bf16[512,128]{1,0:T(8,128)(2,1)S(1)} %collective-permute-done.1.p3), channel_id=1, source_target_pairs={{0,24},{8,0},{16,8},{24,16},{32,56},{40,32},{48,40},{56,48},{64,88... | collective-permute-start | bytes 393224 | tf_op jit(solution)/shard_map/ppermute | solution.py:249
  19.8 10.7 %collective-permute-start.6 = (bf16[128,1024]{1,0:T(8,128)(2,1)S(1)}, bf16[128,1024]{1,0:T(8,128)(2,1)S(1)}, u32[]{:S(2)}, u32[]{:S(2)}) collective-permute-start(bf16[128,1024]{1,0:T(8,128)(2,1)S(1)} %get-tuple-element.55.m0), channel_id=1, source_target_pairs={{0,32},{8,40},{16,48},{24,56},{32,64},{40,72},{48,80},{56,88},{64,... | collective-permute-start | bytes 786440 | tf_op jit(solution)/shard_map/ppermute | solution.py:249
  20.6 9.9 %collective-permute-start.8 = (bf16[128,1024]{1,0:T(8,128)(2,1)S(1)}, bf16[128,1024]{1,0:T(8,128)(2,1)S(1)}, u32[]{:S(2)}, u32[]{:S(2)}) collective-permute-start(bf16[128,1024]{1,0:T(8,128)(2,1)S(1)} %collective-permute-done.7.m3), channel_id=1, source_target_pairs={{0,96},{8,104},{16,112},{24,120},{32,0},{40,8},{48,16},{56,24},{64... | collective-permute-start | bytes 786440 | tf_op jit(solution)/shard_map/ppermute | solution.py:249
  30.9 5.1 %collective-permute-start.11 = (f32[8,1024]{1,0:T(8,128)S(1)}, f32[8,1024]{1,0:T(8,128)S(1)}, u32[]{:S(2)}, u32[]{:S(2)}) collective-permute-start(f32[8,1024]{1,0:T(8,128)S(1)} %get-tuple-element.56.stat_ref.t0), channel_id=1, source_target_pairs={{0,96},{8,104},{16,112},{24,120},{32,0},{40,8},{48,16},{56,24},{64... | collective-permute-start | bytes 98312 | tf_op jit(solution)/shard_map/ppermute | solution.py:249
  32.7 5.5 %collective-permute-start.10 = (f32[8,1024]{1,0:T(8,128)S(1)}, f32[8,1024]{1,0:T(8,128)S(1)}, u32[]{:S(2)}, u32[]{:S(2)}) collective-permute-start(f32[8,1024]{1,0:T(8,128)S(1)} %get-tuple-element.56.stat_ref.t0), channel_id=1, source_target_pairs={{0,64},{8,72},{16,80},{24,88},{32,96},{40,104},{48,112},{56,120},{... | collective-permute-start | bytes 98312 | tf_op jit(solution)/shard_map/ppermute | solution.py:249
  32.7 5.5 %collective-permute-start.9 = (f32[8,1024]{1,0:T(8,128)S(1)}, f32[8,1024]{1,0:T(8,128)S(1)}, u32[]{:S(2)}, u32[]{:S(2)}) collective-permute-start(f32[8,1024]{1,0:T(8,128)S(1)} %get-tuple-element.56.stat_ref.t0), channel_id=1, source_target_pairs={{0,32},{8,40},{16,48},{24,56},{32,64},{40,72},{48,80},{56,88},{64,... | collective-permute-start | bytes 98312 | tf_op jit(solution)/shard_map/ppermute | solution.py:249
  39.1 12.1 %collective-permute-start.12 = (bf16[128,1024]{1,0:T(8,128)(2,1)S(1)}, bf16[128,1024]{1,0:T(8,128)(2,1)S(1)}, u32[]{:S(2)}, u32[]{:S(2)}) collective-permute-start(bf16[128,1024]{1,0:T(8,128)(2,1)S(1)} %get-tuple-element.72), channel_id=1, source_target_pairs={{0,64},{8,72},{16,80},{24,88},{32,96},{40,104},{48,112},{56,120},{... | collective-permute-start | bytes 786440 | tf_op jit(solution)/shard_map/ppermute | solution.py:249
  47.8 5.7 %collective-permute-start.15 = (bf16[512,128]{1,0:T(8,128)(2,1)S(1)}, bf16[512,128]{1,0:T(8,128)(2,1)S(1)}, u32[]{:S(2)}, u32[]{:S(2)}) collective-permute-start(bf16[512,128]{1,0:T(8,128)(2,1)S(1)} %get-tuple-element.76), channel_id=1, source_target_pairs={{0,24},{8,0},{16,8},{24,16},{32,56},{40,32},{48,40},{56,48},{64,88... | collective-permute-start | bytes 393224 | tf_op jit(solution)/shard_map/ppermute | solution.py:249
  49.5 6.9 %collective-permute-start.16 = (bf16[512,128]{1,0:T(8,128)(2,1)S(1)}, bf16[512,128]{1,0:T(8,128)(2,1)S(1)}, u32[]{:S(2)}, u32[]{:S(2)}) collective-permute-start(bf16[512,128]{1,0:T(8,128)(2,1)S(1)} %get-tuple-element.77), channel_id=1, source_target_pairs={{0,8},{8,16},{16,24},{24,0},{32,40},{40,48},{48,56},{56,32},{64,72... | collective-permute-start | bytes 393224 | tf_op jit(solution)/shard_map/ppermute | solution.py:249
  49.8 8.7 %collective-permute-start.17 = (bf16[512,128]{1,0:T(8,128)(2,1)S(1)}, bf16[512,128]{1,0:T(8,128)(2,1)S(1)}, u32[]{:S(2)}, u32[]{:S(2)}) collective-permute-start(bf16[512,128]{1,0:T(8,128)(2,1)S(1)} %get-tuple-element.78), channel_id=1, source_target_pairs={{0,16},{8,24},{16,0},{24,8},{32,48},{40,56},{48,32},{56,40},{64,80... | collective-permute-start | bytes 393224 | tf_op jit(solution)/shard_map/ppermute | solution.py:249
  50.2 9.0 %collective-permute-start.14 = (bf16[128,1024]{1,0:T(8,128)(2,1)S(1)}, bf16[128,1024]{1,0:T(8,128)(2,1)S(1)}, u32[]{:S(2)}, u32[]{:S(2)}) collective-permute-start(bf16[128,1024]{1,0:T(8,128)(2,1)S(1)} %get-tuple-element.74), channel_id=1, source_target_pairs={{0,32},{8,40},{16,48},{24,56},{32,64},{40,72},{48,80},{56,88},{64,... | collective-permute-start | bytes 786440 | tf_op jit(solution)/shard_map/ppermute | solution.py:249
  51.2 8.0 %collective-permute-start.13 = (bf16[128,1024]{1,0:T(8,128)(2,1)S(1)}, bf16[128,1024]{1,0:T(8,128)(2,1)S(1)}, u32[]{:S(2)}, u32[]{:S(2)}) collective-permute-start(bf16[128,1024]{1,0:T(8,128)(2,1)S(1)} %get-tuple-element.73), channel_id=1, source_target_pairs={{0,96},{8,104},{16,112},{24,120},{32,0},{40,8},{48,16},{56,24},{64... | collective-permute-start | bytes 786440 | tf_op jit(solution)/shard_map/ppermute | solution.py:249

commit v3 on v1

v3 whole, which is shorter than its diff:
```python
import functools

import jax
import jax.numpy as jnp
from jax import lax
from jax.experimental import pallas as pl
from jax.experimental.pallas import tpu as pltpu
from jax.sharding import PartitionSpec as P

HEAD_DIM = 128
SIDE = 4
LOG2E = 1.4426950408889634
BF16 = jnp.bfloat16
F32 = jnp.float32


def dot(a, b, ca, cb):
    return lax.dot_general(a, b, (((ca,), (cb,)), ((), ())), preferred_element_type=F32)


def stack_heads(q_ref):
    heads = q_ref.shape[1] // HEAD_DIM
    return jnp.concatenate([q_ref[:, h * HEAD_DIM : (h + 1) * HEAD_DIM] for h in range(heads)], 0)


def prepare_kernel(len_hbm, q_hbm, g_hbm, k_hbm, v_hbm, kr_hbm, vr_hbm,
                   mt_ref, q_ref, kv_ref, kr_ref, vr_ref, g_ref, len_ref, sems):
    piece = k_hbm.shape[0]
    pairs = (
        (len_hbm, len_ref),
        (g_hbm, g_ref),
        (k_hbm, kv_ref.at[pl.ds(0, piece)]),
        (v_hbm, kv_ref.at[pl.ds(piece, piece)]),
        (q_hbm, q_ref),
        (kr_hbm, kr_ref),
        (vr_hbm, vr_ref),
    )
    copies = [pltpu.make_async_copy(a, b, sems.at[n]) for n, (a, b) in enumerate(pairs)]
    for copy in copies:
        copy.start()
    copies[0].wait()
    copies[1].wait()
    rows, cols = g_ref.shape
    alive = lax.broadcasted_iota(jnp.int32, (rows, cols), 0) < len_ref[0]
    masked = jnp.where(alive, g_ref[...].astype(F32), 0.0)
    for h in range(cols // HEAD_DIM):
        part = masked[:, h * HEAD_DIM : (h + 1) * HEAD_DIM]
        mt_ref[:, h * rows : (h + 1) * rows] = part.T.astype(BF16)
    for copy in copies[2:]:
        copy.wait()


def plane_of(pieces, part):
    size = pieces[0].shape[0] // 2
    return jnp.concatenate([p[part * size : (part + 1) * size, :] for p in pieces], 0)


def summary(highest, totals, n, high_ref, lse_ref):
    high = highest * (HEAD_DIM**-0.5 * LOG2E)
    high_ref[n : n + 1, :] = high
    lse_ref[n : n + 1, :] = high + jnp.log2(totals)


def respond(jobs, values, high_ref, lse_ref):
    group, step, small = 16, 256, 64
    scale = HEAD_DIM**-0.5 * LOG2E
    before = None
    for n in range(len(jobs) + 1):
        scoring, weighing = [], []
        if n < len(jobs):
            q_ref, parts, w_ref, a_ref, s_ref = jobs[n]
            q = stack_heads(q_ref)
            wide = q.shape[0]
            top = jnp.full((group, wide), -jnp.inf, F32)
            base = 0
            for keys, mask in parts:
                for r in range(0, keys.shape[0], step):
                    block = keys[r : r + step, :]
                    scoring.append((block, mask, base))
                    base += block.shape[0]
        if n:
            weighing = list(range(0, jobs[n - 1][4].shape[0], small))
            totals = jnp.zeros((group, wide), F32)
        turns = max(len(scoring), 1)
        share = -(-len(weighing) // turns)
        for turn in range(turns):
            if scoring:
                block, mask, base = scoring[turn]
                size = block.shape[0]
                x = dot(block, q, 1, 1)
                if mask is not None:
                    x = jnp.where(mask, x, -jnp.inf)
                jobs[n][4][base : base + size, :] = x
                top = jnp.maximum(top, jnp.max(x.reshape(size // group, group, wide), 0))
            for t in weighing[turn * share : (turn + 1) * share]:
                w = jnp.exp2((jobs[n - 1][4][t : t + small, :] - before) * scale)
                jobs[n - 1][2][t : t + small, :] = w.astype(BF16)
                totals = totals + jnp.sum(w.reshape(small // group, group, wide), 0)
        if n:
            summary(before, jnp.sum(totals, 0, keepdims=True), n - 1, high_ref, lse_ref)
            jobs[n - 1][3][...] = dot(values[n - 1], jobs[n - 1][2][...], 0, 0)
        if n < len(jobs):
            before = jnp.max(top, 0, keepdims=True)


def first_kernel(q0, q1, kr, vr, p0, p1, w0, w1, high_ref, lse_ref, a0, a1, s0, s1):
    rows, wide = kr.shape[0], w1.shape[1]
    keys, values = plane_of((p0, p1), 0), plane_of((p0, p1), 1)
    key_pos = lax.broadcasted_iota(jnp.int32, (rows, wide), 0)
    token = lax.broadcasted_iota(jnp.int32, (rows, wide), 1) % rows
    jobs = (
        (q0, [(kr[...], key_pos <= token), (keys, None)], w0, a0, s0),
        (q1, [(keys, None)], w1, a1, s1),
    )
    respond(jobs, (jnp.concatenate([vr[...], values], 0), values), high_ref, lse_ref)


def second_kernel(q0, q1, q2, q3, p0, p1, p3, p2, w0, w1, w2, w3, high_ref, lse_ref, a0, a1, a2, a3,
                  s0, s1, s2, s3):
    keys, values = plane_of((p3, p2), 0), plane_of((p3, p2), 1)
    pieces = (p0, p1, p3, p2)
    every, all_values = plane_of(pieces, 0), plane_of(pieces, 1)
    jobs = (
        (q0, [(keys, None)], w0, a0, s0),
        (q1, [(keys, None)], w1, a1, s1),
        (q2, [(every, None)], w2, a2, s2),
        (q3, [(every, None)], w3, a3, s3),
    )
    respond(jobs, (values, values, all_values, all_values), high_ref, lse_ref)


def delta_kernel(high01, highs, lse01, lses, a0, a1, b0, b1, b2, b3, m0, m1, m2, m3,
                 high_ref, stat_ref):
    for d, m in enumerate((m0, m1, m2, m3)):
        high_b, lse = highs[d : d + 1, :], lses[d : d + 1, :]
        high_a = high_b
        total = (b0, b1, b2, b3)[d][...]
        if d < 2:
            a = (a0, a1)[d]
            high_a = high01[d : d + 1, :]
            lse_a = lse01[d : d + 1, :]
            top = jnp.maximum(lse, lse_a)
            lse = top + jnp.log2(jnp.exp2(lse - top) + jnp.exp2(lse_a - top))
            total = total * jnp.exp2(high_b - lse) + a[...] * jnp.exp2(high_a - lse)
        else:
            total = total * jnp.exp2(high_b - lse)
        high_ref[2 * d : 2 * d + 1, :] = high_a
        high_ref[2 * d + 1 : 2 * d + 2, :] = high_b
        stat_ref[2 * d : 2 * d + 1, :] = lse
        stat_ref[2 * d + 1 : 2 * d + 2, :] = jnp.sum(m[...].astype(F32) * total, 0, keepdims=True)


def product_kernel(stat_ref, p0, p1, p3, p2, vr, m0, m1, m2, m3, x0, x1, x2, x3, xr):
    values = plane_of((p0, p1, p3, p2), 1)
    for m, x in ((m1, x1), (m3, x3), (m2, x2), (m0, x0)):
        x[...] = dot(values, m[...], 1, 0)
    xr[...] = dot(vr[...], m0[...], 1, 0)


def settle(stats, high_ref, d):
    parts = []
    for e, ref in enumerate(stats):
        row = 2 * ((d - e) % SIDE)
        parts.append((ref[row : row + 1, :], ref[row + 1 : row + 2, :]))
    highest = parts[0][0]
    for lse, term in parts[1:]:
        highest = jnp.maximum(highest, lse)
    totals = jnp.zeros_like(highest)
    delta = jnp.zeros_like(highest)
    for lse, term in parts:
        share = jnp.exp2(lse - highest)
        totals = totals + share
        delta = delta + term * share
    inverse = 1.0 / totals
    factors = jnp.exp2(high_ref[2 * d : 2 * d + 2, :] - highest) * inverse
    return factors, delta * inverse


def turn_back(total, out):
    rows = out.shape[0]
    total = total * HEAD_DIM**-0.5
    for h in range(total.shape[1] // rows):
        part = total[:, h * rows : (h + 1) * rows]
        out[:, h * HEAD_DIM : (h + 1) * HEAD_DIM] = part.T.astype(BF16)


def remote_kernel(t0, t1, t2, t3, high_ref, p0, p1, p3, p2, w2, x2,
                  factor_ref, delta_ref, q2, ds2):
    stats = (t0, t1, t2, t3)
    for d in range(SIDE):
        factors, delta = settle(stats, high_ref, d)
        factor_ref[2 * d : 2 * d + 2, :] = factors
        delta_ref[d : d + 1, :] = delta
        if d == 2:
            ds = w2[...] * ((x2[...] - delta) * factors[0:1, :]).astype(BF16)
            ds2[...] = ds
            turn_back(dot(plane_of((p0, p1, p3, p2), 0), ds, 0, 0), q2)


def local_kernel(factor_ref, delta_ref, p0, p1, p3, p2, kr, w0a, w0b, w1a, w1b, w2, w3,
                 x0, x1, x3, xr, ds2, m0, m1, m2, m3, q0, q1, q2, q3,
                 dq0, dq1, dq3, dkr_ref, dvr_ref, o0, o1, o3, o2):
    rows = kr.shape[0]
    size = p0.shape[0] // 2
    half = w1a.shape[0]
    scale = HEAD_DIM**-0.5
    plane_keys = plane_of((p0, p1, p3, p2), 0)

    def masked(m, d, n):
        return (m[...].astype(F32) * factor_ref[2 * d + n : 2 * d + n + 1, :]).astype(BF16)

    q, g = stack_heads(q2), masked(m2, 2, 0)
    keys = [dot(ds2[n * half : (n + 1) * half, :], q, 1, 0) for n in range(2)]
    values = [dot(w2[n * half : (n + 1) * half, :], g, 1, 1) for n in range(2)]
    for d, q_ref, m, ws, x, out in (
        (1, q1, m1, (w1a, w1b), x1, dq1),
        (3, q3, m3, (w3, w3), x3, dq3),
        (0, q0, m0, (w0a, w0b), x0, dq0),
    ):
        delta = delta_ref[d : d + 1, :]
        q = stack_heads(q_ref)
        grad = None
        for n, w in enumerate(ws):
            factor = factor_ref[2 * d + n : 2 * d + n + 1, :]
            g = masked(m, d, n)
            skip = 0
            if w is w0a:
                skip = rows
                near = w[0:rows, :]
                ds = near * ((xr[...] - delta) * factor).astype(BF16)
                dvr_ref[...] = dot(near, g, 1, 1).astype(BF16)
                dkr_ref[...] = (dot(ds, q, 1, 0) * scale).astype(BF16)
                grad = dot(kr[...], ds, 0, 0)
            here = slice(n * half, (n + 1) * half)
            weights = w[here, :] if w is w3 else w[skip : skip + half, :]
            ds = weights * ((x[here, :] - delta) * factor).astype(BF16)
            values[n] = values[n] + dot(weights, g, 1, 1)
            keys[n] = keys[n] + dot(ds, q, 1, 0)
            part = dot(plane_keys[here, :], ds, 0, 0)
            grad = part if grad is None else grad + part
        turn_back(grad, out)
    for n, outs in enumerate(((o0, o1), (o3, o2))):
        k = (keys[n] * scale).astype(BF16)
        v = values[n].astype(BF16)
        for i, out in enumerate(outs):
            out[0:size, :] = k[i * size : (i + 1) * size, :]
            out[size : 2 * size, :] = v[i * size : (i + 1) * size, :]


def shift_y(d):
    return [(y * SIDE + z, (y + d) % SIDE * SIDE + z) for y in range(SIDE) for z in range(SIDE)]


def shift_z(d):
    return [(y * SIDE + z, y * SIDE + (z + d) % SIDE) for y in range(SIDE) for z in range(SIDE)]


def send(x, perm):
    return lax.ppermute(x, "resp", perm)


def combine(own, received):
    own = own.astype(F32)
    for x in received:
        own = own + x.astype(F32)
    return own.astype(BF16)


def from_others(x, shift):
    one, three, two = (send(x, shift(d)) for d in (1, 3, 2))
    return one, two, three


def call(kernel, name, outs, inputs, memory, scratch=(), flops=0, exps=0, space=pltpu.VMEM):
    return pl.pallas_call(
        kernel,
        out_shape=[jax.ShapeDtypeStruct(*o) for o in outs],
        in_specs=[pl.BlockSpec(memory_space=space)] * len(inputs),
        out_specs=[pl.BlockSpec(memory_space=pltpu.VMEM)] * len(outs),
        scratch_shapes=list(scratch),
        compiler_params=pltpu.CompilerParams(vmem_limit_bytes=memory * 2**20),
        cost_estimate=pl.CostEstimate(flops=flops, bytes_accessed=2**20, transcendentals=exps),
        name=name,
    )(*inputs)


def body(queries, prompt_keys, prompt_values, resp_keys, resp_values, grad_out, lengths):
    rows, cols = queries.shape
    part = prompt_keys.shape[0]
    plane = SIDE * part
    wide = rows * cols // HEAD_DIM
    unit = 2 * wide * plane * HEAD_DIM
    turned = ((HEAD_DIM, wide), BF16)
    turned_wide = ((HEAD_DIM, wide), F32)
    small = ((rows, HEAD_DIM), BF16)
    flat = ((rows, cols), BF16)
    both = ((2 * part, HEAD_DIM), BF16)
    square = ((plane, wide), BF16)
    square_wide = ((plane, wide), F32)

    q1, q3 = (send(queries, shift_y(d)) for d in (1, 3))
    params = (queries, grad_out, prompt_keys, prompt_values, resp_keys, resp_values)
    m0, q0, piece, kr, vr = call(
        prepare_kernel, "prepare", [turned, flat, both, small, small],
        [lengths] + [pltpu.with_memory_space_constraint(x, pltpu.HBM) for x in params], 8,
        [pltpu.VMEM((rows, cols), BF16), pltpu.SMEM((1,), jnp.int32),
         pltpu.SemaphoreType.DMA((7,))], space=pltpu.HBM)
    p1, p3 = (send(piece, shift_z(d)) for d in (1, 3))
    pieces = (piece, p1, p3, send(p3, shift_z(3)))
    later, unused = lax.optimization_barrier((q1, p1))
    q2 = send(later, shift_y(1))
    m1, m3 = (send(m0, shift_y(d)) for d in (1, 3))
    m2 = send(m3, shift_y(3))
    half = plane // 2
    tall, short = ((half + rows, wide), BF16), ((half, wide), BF16)
    line = ((2, wide), F32)
    w0a, w1a, high01, lse01, a0, a1 = call(
        first_kernel, "first", [tall, short, line, line] + [turned_wide] * 2,
        (q0, q1, kr, vr, piece, p1), 16,
        [pltpu.VMEM(x[0], F32) for x in (tall, short)], flops=3 * unit, exps=plane * wide)
    w0b, w1b, w2, w3, highs, lses, b0, b1, b2, b3 = call(
        second_kernel, "second",
        [short, short, square, square] + [((SIDE, wide), F32)] * 2 + [turned_wide] * 4,
        (q0, q1, q2, q3, *pieces), 24,
        [pltpu.VMEM(x[0], F32) for x in (short, short, square, square)], flops=6 * unit,
        exps=3 * plane * wide)
    high, stat = call(
        delta_kernel, "delta", [((2 * SIDE, wide), F32)] * 2,
        (high01, highs, lse01, lses, a0, a1, b0, b1, b2, b3, m0, m1, m2, m3), 8,
        flops=unit // 2)
    all_stats = (stat, *from_others(stat, shift_y))
    x0, x1, x2, x3, xr = call(
        product_kernel, "product", [square_wide] * 4 + [((rows, wide), F32)],
        (stat, *pieces, vr, m0, m1, m2, m3), 12, flops=4 * unit)
    factors, delta, dq2, ds2 = call(
        remote_kernel, "remote",
        [((2 * SIDE, wide), F32), ((SIDE, wide), F32), flat, square],
        (*all_stats, high, *pieces, w2, x2), 12, flops=unit)
    back2 = send(dq2, shift_y(-2))
    dq0, dq1, dq3, dkr, dvr, o0, o1, o3, o2 = call(
        local_kernel, "local", [flat] * 3 + [small, small] + [both] * 4,
        (factors, delta, *pieces, kr, w0a, w0b, w1a, w1b, w2, w3, x0, x1, x3, xr, ds2,
         m0, m1, m2, m3, q0, q1, q2, q3), 16, flops=11 * unit)
    dq1, unused = lax.optimization_barrier((dq1, back2))
    total = combine(o0, [send(x, shift_z(-d)) for d, x in ((2, o2), (1, o1), (3, o3))])
    returned = [send(x, shift_y(-d)) for d, x in ((1, dq1), (3, dq3))] + [back2]
    grad_queries = combine(dq0, returned)
    return grad_queries, total[:part], total[part:], dkr, dvr


def solution(mesh):
    spec = P(("group", "resp"), "tp")
    return jax.shard_map(
        body,
        mesh=mesh,
        in_specs=(spec,) * 6 + (P(("group", "resp")),),
        out_specs=(spec,) * 5,
        check_vma=False,
    )
```

time: 63 us -> 60.2 us (0.956)
  the two profiles are of different devices: /device:TPU:2 before, /device:TPU:40 now
where the time goes in v3:
time: 60.2 us; the launch traced here: 60.1 us
  starting transfers between devices  27.2 us (45%)
  Pallas kernels  18.6 us (31%)
  waiting for transfers between devices  11.3 us (19%)
  between operations  1.39 us (2%)
  other arithmetic  0.94 us (2%)
  local copies, waits for them, and re-layouts  0.66 us (1%)
    ppermute x18, starting transfers between devices, send(): return lax.ppermute(x, 'resp', perm)  27.2 us
    pallas_call x7, Pallas kernels, call(): pl.pallas_call(kernel, out_shape=[jax.ShapeDtypeStruct(*o) for o in outs]...  18.6 us
    ppermute x18, waiting for transfers between devices, send(): return lax.ppermute(x, 'resp', perm)  11.3 us
  transfers between devices with their start and end apart: 18, of which 6 were waited for; matrix products, arithmetic and copies ran while one was open for 1% of the time, Pallas kernels for 28%

profile of v3, /device:TPU:40, one launch (start us, length us, event | category | flops | bytes accessed | tf_op | source)
XLA Modules:
  0.0 60.1 jit_solution(1010871194256597921)
XLA Ops:
  0.6 1.7 %collective-permute-start = (bf16[128,1024]{1,0:T(8,128)(2,1)}, bf16[128,1024]{1,0:T(8,128)(2,1)S(1)}, u32[]{:S(2)}, u32[]{:S(2)}) collective-permute-start(bf16[128,1024]{1,0:T(8,128)(2,1)} %q_hbm.1), channel_id=1, source_target_pairs={{0,32},{8,40},{16,48},{24,56},{32,64},{40,72},{48,80},{56,88},{64,... | collective-permute-start | bytes 786440 | tf_op jit(solution)/shard_map/ppermute | solution.py:259
  2.9 1.2 %prepare.1 = (bf16[128,1024]{1,0:T(8,128)(2,1)S(1)}, bf16[128,1024]{1,0:T(8,128)(2,1)S(1)}, bf16[512,128]{1,0:T(8,128)(2,1)S(1)}, bf16[128,128]{1,0:T(8,128)(2,1)S(1)}, bf16[128,128]{1,0:T(8,128)(2,1)S(1)}) custom-call(s32[1]{0:T(128)S(6)} %copy.12.len_hbm, bf16[128,1024]{1,0:T(8,128)(2,1)} %q_hbm.1, bf16[128,1024]{1,0:T(8,128)(2,1)} %g_hbm.1, ...), custom_call_target="tpu_custom_call" | custom-call | bytes 1048576 | tf_op jit(solution)/shard_map/prepare/pallas_call | solution.py:275
  4.1 2.0 %collective-permute-start.1 = (bf16[512,128]{1,0:T(8,128)(2,1)S(1)}, bf16[512,128]{1,0:T(8,128)(2,1)S(1)}, u32[]{:S(2)}, u32[]{:S(2)}) collective-permute-start(bf16[512,128]{1,0:T(8,128)(2,1)S(1)} %get-tuple-element.51.p0), channel_id=1, source_target_pairs={{0,8},{8,16},{16,24},{24,0},{32,40},{40,48},{48,56},{56,32},{64,72... | collective-permute-start | bytes 393224 | tf_op jit(solution)/shard_map/ppermute | solution.py:259
  6.1 0.5 collective-permute-start.7
  6.6 1.7 %collective-permute-start.3 = (bf16[128,1024]{1,0:T(8,128)(2,1)}, bf16[128,1024]{1,0:T(8,128)(2,1)S(1)}, u32[]{:S(2)}, u32[]{:S(2)}) collective-permute-start(bf16[128,1024]{1,0:T(8,128)(2,1)} %q_hbm.1), channel_id=1, source_target_pairs={{0,96},{8,104},{16,112},{24,120},{32,0},{40,8},{48,16},{56,24},{64... | collective-permute-start | bytes 786440 | tf_op jit(solution)/shard_map/ppermute | solution.py:259
  8.2 0.1 collective-permute-start.4
  8.3 0.8 %collective-permute-done.1.p1 = bf16[512,128]{1,0:T(8,128)(2,1)S(1)} collective-permute-done((bf16[512,128]{1,0:T(8,128)(2,1)S(1)}, bf16[512,128]{1,0:T(8,128)(2,1)S(1)}, u32[]{:S(2)}, u32[]{:S(2)}) %collective-permute-start.1) | collective-permute-done | bytes 131104 | tf_op jit(solution)/shard_map/ppermute | solution.py:259
  9.2 0.0 collective-permute-done.q1
  9.2 1.4 %collective-permute-start.2 = (bf16[128,1024]{1,0:T(8,128)(2,1)S(1)}, bf16[128,1024]{1,0:T(8,128)(2,1)S(1)}, u32[]{:S(2)}, u32[]{:S(2)}) collective-permute-start(bf16[128,1024]{1,0:T(8,128)(2,1)S(1)} %collective-permute-done.q1), channel_id=1, source_target_pairs={{0,32},{8,40},{16,48},{24,56},{32,64},{40,72},{48,80},{56,88},{64,... | collective-permute-start | bytes 786440 | tf_op jit(solution)/shard_map/ppermute | solution.py:259
  10.5 2.9 %collective-permute-done.4.p3 = bf16[512,128]{1,0:T(8,128)(2,1)S(1)} collective-permute-done((bf16[512,128]{1,0:T(8,128)(2,1)S(1)}, bf16[512,128]{1,0:T(8,128)(2,1)S(1)}, u32[]{:S(2)}, u32[]{:S(2)}) %collective-permute-start.4) | collective-permute-done | bytes 131104 | tf_op jit(solution)/shard_map/ppermute | solution.py:259
  13.5 1.5 %collective-permute-start.5 = (bf16[512,128]{1,0:T(8,128)(2,1)S(1)}, bf16[512,128]{1,0:T(8,128)(2,1)S(1)}, u32[]{:S(2)}, u32[]{:S(2)}) collective-permute-start(bf16[512,128]{1,0:T(8,128)(2,1)S(1)} %collective-permute-done.4.p3), channel_id=1, source_target_pairs={{0,24},{8,0},{16,8},{24,16},{32,56},{40,32},{48,40},{56,48},{64,88... | collective-permute-start | bytes 393224 | tf_op jit(solution)/shard_map/ppermute | solution.py:259
  14.9 0.8 %collective-permute-start.6 = (bf16[128,1024]{1,0:T(8,128)(2,1)S(1)}, bf16[128,1024]{1,0:T(8,128)(2,1)S(1)}, u32[]{:S(2)}, u32[]{:S(2)}) collective-permute-start(bf16[128,1024]{1,0:T(8,128)(2,1)S(1)} %get-tuple-element.63.m0), channel_id=1, source_target_pairs={{0,32},{8,40},{16,48},{24,56},{32,64},{40,72},{48,80},{56,88},{64,... | collective-permute-start | bytes 786440 | tf_op jit(solution)/shard_map/ppermute | solution.py:259
  15.8 0.0 collective-permute-done.7.m3
  15.8 1.2 %collective-permute-start.8 = (bf16[128,1024]{1,0:T(8,128)(2,1)S(1)}, bf16[128,1024]{1,0:T(8,128)(2,1)S(1)}, u32[]{:S(2)}, u32[]{:S(2)}) collective-permute-start(bf16[128,1024]{1,0:T(8,128)(2,1)S(1)} %collective-permute-done.7.m3), channel_id=1, source_target_pairs={{0,96},{8,104},{16,112},{24,120},{32,0},{40,8},{48,16},{56,24},{64... | collective-permute-start | bytes 786440 | tf_op jit(solution)/shard_map/ppermute | solution.py:259
  17.0 2.1 %first.1 = (bf16[640,1024]{1,0:T(8,128)(2,1)S(1)}, bf16[512,1024]{1,0:T(8,128)(2,1)S(1)}, f32[2,1024]{1,0:T(2,128)S(1)}, f32[2,1024]{1,0:T(2,128)S(1)}, f32[128,...) custom-call(bf16[128,1024]{1,0:T(8,128)(2,1)S(1)} %get-tuple-element.48.q0, bf16[128,1024]{1,0:T(8,128)(2,1)S(1)} %collective-permute-done.q1, ...), custom_call_target="tpu_custom_call" | custom-call | flops 805306368 | bytes 1048576 | tf_op jit(solution)/shard_map/first/pallas_call | solution.py:275
  19.1 1.9 %collective-permute-done.3.q3 = bf16[128,1024]{1,0:T(8,128)(2,1)S(1)} collective-permute-done((bf16[128,1024]{1,0:T(8,128)(2,1)}, bf16[128,1024]{1,0:T(8,128)(2,1)S(1)}, u32[]{:S(2)}, u32[]{:S(2)}) %collective-permute-start.3) | collective-permute-done | bytes 262176 | tf_op jit(solution)/shard_map/ppermute | solution.py:259
  21.0 0.0 collective-permute-done.5.p2
  21.0 0.0 collective-permute-done.2.q2
  21.0 5.3 %second.1 = (bf16[512,1024]{1,0:T(8,128)(2,1)S(1)}, bf16[512,1024]{1,0:T(8,128)(2,1)S(1)}, bf16[1024,1024]{1,0:T(8,128)(2,1)S(1)}, bf16[1024,1024]{1,0:T(8,128)(...) custom-call(bf16[128,1024]{1,0:T(8,128)(2,1)S(1)} %get-tuple-element, ...), custom_call_target="tpu_custom_call" | custom-call | flops 1610612736 | bytes 1048576 | tf_op jit(solution)/shard_map/second/pallas_call | solution.py:275
  26.3 0.0 collective-permute-done.6.m1
  26.3 0.0 collective-permute-done.8.m2
  26.3 0.6 %delta.1 = (f32[8,1024]{1,0:T(8,128)S(1)}, f32[8,1024]{1,0:T(8,128)S(1)}) custom-call(f32[2,1024]{1,0:T(2,128)S(1)} %get-tuple-element.52.high01, f32[4,1024]{1,0:T(4,128)S(1)} %get-tuple-element.54.highs, f32[2,1024]{1,0:T(2,128)S(1)} %get-tuple-element.55.lse01, f32[4,1024]{1,0:T(4,128)S(1)} %get-tuple-element.56.lses, ...), custom_call_target="tpu_custom_call" | custom-call | flops 134217728 | bytes 1048576 | tf_op jit(solution)/shard_map/delta/pallas_call | solution.py:275
  26.9 0.1 collective-permute-start.11
  27.0 2.7 %collective-permute-start.10 = (f32[8,1024]{1,0:T(8,128)S(1)}, f32[8,1024]{1,0:T(8,128)S(1)}, u32[]{:S(2)}, u32[]{:S(2)}) collective-permute-start(f32[8,1024]{1,0:T(8,128)S(1)} %get-tuple-element.64.stat_ref.t0), channel_id=1, source_target_pairs={{0,64},{8,72},{16,80},{24,88},{32,96},{40,104},{48,112},{56,120},{... | collective-permute-start | bytes 98312 | tf_op jit(solution)/shard_map/ppermute | solution.py:259
  29.8 2.0 %collective-permute-start.9 = (f32[8,1024]{1,0:T(8,128)S(1)}, f32[8,1024]{1,0:T(8,128)S(1)}, u32[]{:S(2)}, u32[]{:S(2)}) collective-permute-start(f32[8,1024]{1,0:T(8,128)S(1)} %get-tuple-element.64.stat_ref.t0), channel_id=1, source_target_pairs={{0,32},{8,40},{16,48},{24,56},{32,64},{40,72},{48,80},{56,88},{64,... | collective-permute-start | bytes 98312 | tf_op jit(solution)/shard_map/ppermute | solution.py:259
  31.8 2.4 %product.1 = (f32[1024,1024]{1,0:T(8,128)S(1)}, f32[1024,1024]{1,0:T(8,128)S(1)}, f32[1024,1024]{1,0:T(8,128)S(1)}, f32[1024,1024]{1,0:T(8,128)S(1)}, f32[128,1024]{1,0:T(8,128)S(1)}) custom-call(f32[8,1024]{1,0:T(8,128)S(1)} %get-tuple-element.64.stat_ref.t0, bf16[512,128]{1,0:T(8,128)(2,1)S(1)} %get-tuple-element.51.p0, ...), custom_call_target="tpu_custom_call" | custom-call | flops 1073741824 | bytes 1048576 | tf_op jit(solution)/shard_map/product/pallas_call | solution.py:275
  34.2 0.0 collective-permute-done.11.t3
  34.2 0.0 collective-permute-done.10.t2
  34.2 0.0 collective-permute-done.9.t1
  34.2 0.9 %remote.1 = (f32[8,1024]{1,0:T(8,128)S(1)}, f32[4,1024]{1,0:T(4,128)S(1)}, bf16[128,1024]{1,0:T(8,128)(2,1)S(1)}, bf16[1024,1024]{1,0:T(8,128)(2,1)S(1)}) custom-call(f32[8,1024]{1,0:T(8,128)S(1)} %get-tuple-element.64.stat_ref.t0, f32[8,1024]{1,0:T(8,128)S(1)} %collective-permute-done.9.t1, f32[8,1024]{1,0:T(8,128)S(1)} %collective-permute-done.10.t2, ...), custom_call_target="tpu_custom_call" | custom-call | flops 268435456 | bytes 1048576 | tf_op jit(solution)/shard_map/remote/pallas_call | solution.py:275
  35.2 1.7 %collective-permute-start.12 = (bf16[128,1024]{1,0:T(8,128)(2,1)S(1)}, bf16[128,1024]{1,0:T(8,128)(2,1)S(1)}, u32[]{:S(2)}, u32[]{:S(2)}) collective-permute-start(bf16[128,1024]{1,0:T(8,128)(2,1)S(1)} %get-tuple-element.82), channel_id=1, source_target_pairs={{0,64},{8,72},{16,80},{24,88},{32,96},{40,104},{48,112},{56,120},{... | collective-permute-start | bytes 786440 | tf_op jit(solution)/shard_map/ppermute | solution.py:259
  36.9 6.0 %local.1 = (bf16[128,1024]{1,0:T(8,128)(2,1)S(1)}, bf16[128,1024]{1,0:T(8,128)(2,1)S(1)}, bf16[128,1024]{1,0:T(8,128)(2,1)S(1)}, bf16[128,128]{1,0:T(8,128)(2,1)...) custom-call(f32[8,1024]{1,0:T(8,128)S(1)} %get-tuple-element.68.fact, ...), custom_call_target="tpu_custom_call" | custom-call | flops 2952790016 | bytes 1048576 | tf_op jit(solution)/shard_map/local/pallas_call | solution.py:275
  42.9 3.1 %collective-permute-start.15 = (bf16[512,128]{1,0:T(8,128)(2,1)S(1)}, bf16[512,128]{1,0:T(8,128)(2,1)S(1)}, u32[]{:S(2)}, u32[]{:S(2)}) collective-permute-start(bf16[512,128]{1,0:T(8,128)(2,1)S(1)} %get-tuple-element.86), channel_id=1, source_target_pairs={{0,16},{8,24},{16,0},{24,8},{32,48},{40,56},{48,32},{56,40},{64,80... | collective-permute-start | bytes 393224 | tf_op jit(solution)/shard_map/ppermute | solution.py:259
  46.0 0.3 collective-permute-start.16
  46.3 1.7 %collective-permute-start.17 = (bf16[512,128]{1,0:T(8,128)(2,1)S(1)}, bf16[512,128]{1,0:T(8,128)(2,1)S(1)}, u32[]{:S(2)}, u32[]{:S(2)}) collective-permute-start(bf16[512,128]{1,0:T(8,128)(2,1)S(1)} %get-tuple-element.88), channel_id=1, source_target_pairs={{0,8},{8,16},{16,24},{24,0},{32,40},{40,48},{48,56},{56,32},{64,72... | collective-permute-start | bytes 393224 | tf_op jit(solution)/shard_map/ppermute | solution.py:259
  48.0 4.8 %collective-permute-start.14 = (bf16[128,1024]{1,0:T(8,128)(2,1)S(1)}, bf16[128,1024]{1,0:T(8,128)(2,1)S(1)}, u32[]{:S(2)}, u32[]{:S(2)}) collective-permute-start(bf16[128,1024]{1,0:T(8,128)(2,1)S(1)} %get-tuple-element.84), channel_id=1, source_target_pairs={{0,32},{8,40},{16,48},{24,56},{32,64},{40,72},{48,80},{56,88},{64,... | collective-permute-start | bytes 786440 | tf_op jit(solution)/shard_map/ppermute | solution.py:259
  52.8 0.0 collective-permute-done.12
  52.8 0.0 collective-permute-start.13
  52.8 0.0 collective-permute-done.15
  52.9 1.1 %collective-permute-done.16 = bf16[512,128]{1,0:T(8,128)(2,1)S(1)} collective-permute-done((bf16[512,128]{1,0:T(8,128)(2,1)S(1)}, bf16[512,128]{1,0:T(8,128)(2,1)S(1)}, u32[]{:S(2)}, u32[]{:S(2)}) %collective-permute-start.16) | collective-permute-done | bytes 131104 | tf_op jit(solution)/shard_map/ppermute | solution.py:259
  53.9 0.0 collective-permute-done.17
  53.9 0.1 add_convert_fusion.1
  54.0 0.7 %fusion = (bf16[256,128]{1,0:T(8,128)(2,1)}, bf16[256,128]{1,0:T(8,128)(2,1)}) fusion(bf16[512,128]{1,0:T(8,128)(2,1)S(1)} %add_convert_fusion.1), kind=kLoop, calls=%fused_computation.2 | loop fusion | bytes 262144 | tf_op jit(solution)/shard_map/slice | solution.py:348
  54.6 2.1 %collective-permute-done.14 = bf16[128,1024]{1,0:T(8,128)(2,1)S(1)} collective-permute-done((bf16[128,1024]{1,0:T(8,128)(2,1)S(1)}, bf16[128,1024]{1,0:T(8,128)(2,1)S(1)}, u32[]{:S(2)}, u32[]{:S(2)}) %collective-permute-start.14) | collective-permute-done | bytes 262176 | tf_op jit(solution)/shard_map/ppermute | solution.py:259
  56.7 2.5 %collective-permute-done.13 = bf16[128,1024]{1,0:T(8,128)(2,1)S(1)} collective-permute-done((bf16[128,1024]{1,0:T(8,128)(2,1)S(1)}, bf16[128,1024]{1,0:T(8,128)(2,1)S(1)}, u32[]{:S(2)}, u32[]{:S(2)}) %collective-permute-start.13) | collective-permute-done | bytes 262176 | tf_op jit(solution)/shard_map/ppermute | solution.py:259
  59.2 0.9 %add_convert_fusion = bf16[128,1024]{1,0:T(8,128)(2,1)} fusion(bf16[128,1024]{1,0:T(8,128)(2,1)S(1)} %collective-permute-done.12, bf16[128,1024]{1,0:T(8,128)(2,1)S(1)} %collective-permute-done.14, bf16[128,1024]{1,0:T(8,128)(2,1)S(1)} %collective-permute-done.13, bf16[128,1024]{1,0:T(8,128)(2,1)S(1)} %get-tuple-element.80), kind=kLoop, calls=%fused_computation | loop fusion | flops 1048576 | bytes 1310720 | tf_op jit(solution)/shard_map/convert_element_type | solution.py:266
Async XLA Ops:
  0.6 8.5 %collective-permute-start = (bf16[128,1024]{1,0:T(8,128)(2,1)}, bf16[128,1024]{1,0:T(8,128)(2,1)S(1)}, u32[]{:S(2)}, u32[]{:S(2)}) collective-permute-start(bf16[128,1024]{1,0:T(8,128)(2,1)} %q_hbm.1), channel_id=1, source_target_pairs={{0,32},{8,40},{16,48},{24,56},{32,64},{40,72},{48,80},{56,88},{64,... | collective-permute-start | bytes 786440 | tf_op jit(solution)/shard_map/ppermute | solution.py:259
  4.1 5.0 %collective-permute-start.1 = (bf16[512,128]{1,0:T(8,128)(2,1)S(1)}, bf16[512,128]{1,0:T(8,128)(2,1)S(1)}, u32[]{:S(2)}, u32[]{:S(2)}) collective-permute-start(bf16[512,128]{1,0:T(8,128)(2,1)S(1)} %get-tuple-element.51.p0), channel_id=1, source_target_pairs={{0,8},{8,16},{16,24},{24,0},{32,40},{40,48},{48,56},{56,32},{64,72... | collective-permute-start | bytes 393224 | tf_op jit(solution)/shard_map/ppermute | solution.py:259
  6.1 9.7 %collective-permute-start.7 = (bf16[128,1024]{1,0:T(8,128)(2,1)S(1)}, bf16[128,1024]{1,0:T(8,128)(2,1)S(1)}, u32[]{:S(2)}, u32[]{:S(2)}) collective-permute-start(bf16[128,1024]{1,0:T(8,128)(2,1)S(1)} %get-tuple-element.63.m0), channel_id=1, source_target_pairs={{0,96},{8,104},{16,112},{24,120},{32,0},{40,8},{48,16},{56,24},{64... | collective-permute-start | bytes 786440 | tf_op jit(solution)/shard_map/ppermute | solution.py:259
  6.6 14.4 %collective-permute-start.3 = (bf16[128,1024]{1,0:T(8,128)(2,1)}, bf16[128,1024]{1,0:T(8,128)(2,1)S(1)}, u32[]{:S(2)}, u32[]{:S(2)}) collective-permute-start(bf16[128,1024]{1,0:T(8,128)(2,1)} %q_hbm.1), channel_id=1, source_target_pairs={{0,96},{8,104},{16,112},{24,120},{32,0},{40,8},{48,16},{56,24},{64... | collective-permute-start | bytes 786440 | tf_op jit(solution)/shard_map/ppermute | solution.py:259
  8.2 5.3 %collective-permute-start.4 = (bf16[512,128]{1,0:T(8,128)(2,1)S(1)}, bf16[512,128]{1,0:T(8,128)(2,1)S(1)}, u32[]{:S(2)}, u32[]{:S(2)}) collective-permute-start(bf16[512,128]{1,0:T(8,128)(2,1)S(1)} %get-tuple-element.51.p0), channel_id=1, source_target_pairs={{0,24},{8,0},{16,8},{24,16},{32,56},{40,32},{48,40},{56,48},{64,88... | collective-permute-start | bytes 393224 | tf_op jit(solution)/shard_map/ppermute | solution.py:259
  9.2 11.8 %collective-permute-start.2 = (bf16[128,1024]{1,0:T(8,128)(2,1)S(1)}, bf16[128,1024]{1,0:T(8,128)(2,1)S(1)}, u32[]{:S(2)}, u32[]{:S(2)}) collective-permute-start(bf16[128,1024]{1,0:T(8,128)(2,1)S(1)} %collective-permute-done.q1), channel_id=1, source_target_pairs={{0,32},{8,40},{16,48},{24,56},{32,64},{40,72},{48,80},{56,88},{64,... | collective-permute-start | bytes 786440 | tf_op jit(solution)/shard_map/ppermute | solution.py:259
  13.5 7.5 %collective-permute-start.5 = (bf16[512,128]{1,0:T(8,128)(2,1)S(1)}, bf16[512,128]{1,0:T(8,128)(2,1)S(1)}, u32[]{:S(2)}, u32[]{:S(2)}) collective-permute-start(bf16[512,128]{1,0:T(8,128)(2,1)S(1)} %collective-permute-done.4.p3), channel_id=1, source_target_pairs={{0,24},{8,0},{16,8},{24,16},{32,56},{40,32},{48,40},{56,48},{64,88... | collective-permute-start | bytes 393224 | tf_op jit(solution)/shard_map/ppermute | solution.py:259
  14.9 11.3 %collective-permute-start.6 = (bf16[128,1024]{1,0:T(8,128)(2,1)S(1)}, bf16[128,1024]{1,0:T(8,128)(2,1)S(1)}, u32[]{:S(2)}, u32[]{:S(2)}) collective-permute-start(bf16[128,1024]{1,0:T(8,128)(2,1)S(1)} %get-tuple-element.63.m0), channel_id=1, source_target_pairs={{0,32},{8,40},{16,48},{24,56},{32,64},{40,72},{48,80},{56,88},{64,... | collective-permute-start | bytes 786440 | tf_op jit(solution)/shard_map/ppermute | solution.py:259
  15.8 10.5 %collective-permute-start.8 = (bf16[128,1024]{1,0:T(8,128)(2,1)S(1)}, bf16[128,1024]{1,0:T(8,128)(2,1)S(1)}, u32[]{:S(2)}, u32[]{:S(2)}) collective-permute-start(bf16[128,1024]{1,0:T(8,128)(2,1)S(1)} %collective-permute-done.7.m3), channel_id=1, source_target_pairs={{0,96},{8,104},{16,112},{24,120},{32,0},{40,8},{48,16},{56,24},{64... | collective-permute-start | bytes 786440 | tf_op jit(solution)/shard_map/ppermute | solution.py:259
  26.9 7.3 %collective-permute-start.11 = (f32[8,1024]{1,0:T(8,128)S(1)}, f32[8,1024]{1,0:T(8,128)S(1)}, u32[]{:S(2)}, u32[]{:S(2)}) collective-permute-start(f32[8,1024]{1,0:T(8,128)S(1)} %get-tuple-element.64.stat_ref.t0), channel_id=1, source_target_pairs={{0,96},{8,104},{16,112},{24,120},{32,0},{40,8},{48,16},{56,24},{64... | collective-permute-start | bytes 98312 | tf_op jit(solution)/shard_map/ppermute | solution.py:259
  27.0 7.2 %collective-permute-start.10 = (f32[8,1024]{1,0:T(8,128)S(1)}, f32[8,1024]{1,0:T(8,128)S(1)}, u32[]{:S(2)}, u32[]{:S(2)}) collective-permute-start(f32[8,1024]{1,0:T(8,128)S(1)} %get-tuple-element.64.stat_ref.t0), channel_id=1, source_target_pairs={{0,64},{8,72},{16,80},{24,88},{32,96},{40,104},{48,112},{56,120},{... | collective-permute-start | bytes 98312 | tf_op jit(solution)/shard_map/ppermute | solution.py:259
  29.8 4.5 %collective-permute-start.9 = (f32[8,1024]{1,0:T(8,128)S(1)}, f32[8,1024]{1,0:T(8,128)S(1)}, u32[]{:S(2)}, u32[]{:S(2)}) collective-permute-start(f32[8,1024]{1,0:T(8,128)S(1)} %get-tuple-element.64.stat_ref.t0), channel_id=1, source_target_pairs={{0,32},{8,40},{16,48},{24,56},{32,64},{40,72},{48,80},{56,88},{64,... | collective-permute-start | bytes 98312 | tf_op jit(solution)/shard_map/ppermute | solution.py:259
  35.2 17.7 %collective-permute-start.12 = (bf16[128,1024]{1,0:T(8,128)(2,1)S(1)}, bf16[128,1024]{1,0:T(8,128)(2,1)S(1)}, u32[]{:S(2)}, u32[]{:S(2)}) collective-permute-start(bf16[128,1024]{1,0:T(8,128)(2,1)S(1)} %get-tuple-element.82), channel_id=1, source_target_pairs={{0,64},{8,72},{16,80},{24,88},{32,96},{40,104},{48,112},{56,120},{... | collective-permute-start | bytes 786440 | tf_op jit(solution)/shard_map/ppermute | solution.py:259
  42.9 10.0 %collective-permute-start.15 = (bf16[512,128]{1,0:T(8,128)(2,1)S(1)}, bf16[512,128]{1,0:T(8,128)(2,1)S(1)}, u32[]{:S(2)}, u32[]{:S(2)}) collective-permute-start(bf16[512,128]{1,0:T(8,128)(2,1)S(1)} %get-tuple-element.86), channel_id=1, source_target_pairs={{0,16},{8,24},{16,0},{24,8},{32,48},{40,56},{48,32},{56,40},{64,80... | collective-permute-start | bytes 393224 | tf_op jit(solution)/shard_map/ppermute | solution.py:259
  46.0 7.9 %collective-permute-start.16 = (bf16[512,128]{1,0:T(8,128)(2,1)S(1)}, bf16[512,128]{1,0:T(8,128)(2,1)S(1)}, u32[]{:S(2)}, u32[]{:S(2)}) collective-permute-start(bf16[512,128]{1,0:T(8,128)(2,1)S(1)} %get-tuple-element.87), channel_id=1, source_target_pairs={{0,24},{8,0},{16,8},{24,16},{32,56},{40,32},{48,40},{56,48},{64,88... | collective-permute-start | bytes 393224 | tf_op jit(solution)/shard_map/ppermute | solution.py:259
  46.3 7.7 %collective-permute-start.17 = (bf16[512,128]{1,0:T(8,128)(2,1)S(1)}, bf16[512,128]{1,0:T(8,128)(2,1)S(1)}, u32[]{:S(2)}, u32[]{:S(2)}) collective-permute-start(bf16[512,128]{1,0:T(8,128)(2,1)S(1)} %get-tuple-element.88), channel_id=1, source_target_pairs={{0,8},{8,16},{16,24},{24,0},{32,40},{40,48},{48,56},{56,32},{64,72... | collective-permute-start | bytes 393224 | tf_op jit(solution)/shard_map/ppermute | solution.py:259
  48.0 8.7 %collective-permute-start.14 = (bf16[128,1024]{1,0:T(8,128)(2,1)S(1)}, bf16[128,1024]{1,0:T(8,128)(2,1)S(1)}, u32[]{:S(2)}, u32[]{:S(2)}) collective-permute-start(bf16[128,1024]{1,0:T(8,128)(2,1)S(1)} %get-tuple-element.84), channel_id=1, source_target_pairs={{0,32},{8,40},{16,48},{24,56},{32,64},{40,72},{48,80},{56,88},{64,... | collective-permute-start | bytes 786440 | tf_op jit(solution)/shard_map/ppermute | solution.py:259
  52.8 6.4 %collective-permute-start.13 = (bf16[128,1024]{1,0:T(8,128)(2,1)S(1)}, bf16[128,1024]{1,0:T(8,128)(2,1)S(1)}, u32[]{:S(2)}, u32[]{:S(2)}) collective-permute-start(bf16[128,1024]{1,0:T(8,128)(2,1)S(1)} %get-tuple-element.83), channel_id=1, source_target_pairs={{0,96},{8,104},{16,112},{24,120},{32,0},{40,8},{48,16},{56,24},{64... | collective-permute-start | bytes 786440 | tf_op jit(solution)/shard_map/ppermute | solution.py:259

commit v4 on v3

--- a/solution.py
+++ b/solution.py
@@ -184,22 +184,13 @@
         out[:, h * HEAD_DIM : (h + 1) * HEAD_DIM] = part.T.astype(BF16)
 
 
-def remote_kernel(t0, t1, t2, t3, high_ref, p0, p1, p3, p2, w2, x2,
-                  factor_ref, delta_ref, q2, ds2):
-    stats = (t0, t1, t2, t3)
+def local_kernel(t0, t1, t2, t3, high_ref, p0, p1, p3, p2, kr, w0a, w0b, w1a, w1b, w2, w3,
+                 x0, x1, x2, x3, xr, m0, m1, m2, m3, q0, q1, q2, q3,
+                 dq0, dq1, dq2, dq3, dkr_ref, dvr_ref, o0, o1, o3, o2, factor_ref, delta_ref):
     for d in range(SIDE):
-        factors, delta = settle(stats, high_ref, d)
+        factors, delta = settle((t0, t1, t2, t3), high_ref, d)
         factor_ref[2 * d : 2 * d + 2, :] = factors
         delta_ref[d : d + 1, :] = delta
-        if d == 2:
-            ds = w2[...] * ((x2[...] - delta) * factors[0:1, :]).astype(BF16)
-            ds2[...] = ds
-            turn_back(dot(plane_of((p0, p1, p3, p2), 0), ds, 0, 0), q2)
-
-
-def local_kernel(factor_ref, delta_ref, p0, p1, p3, p2, kr, w0a, w0b, w1a, w1b, w2, w3,
-                 x0, x1, x3, xr, ds2, m0, m1, m2, m3, q0, q1, q2, q3,
-                 dq0, dq1, dq3, dkr_ref, dvr_ref, o0, o1, o3, o2):
     rows = kr.shape[0]
     size = p0.shape[0] // 2
     half = w1a.shape[0]
@@ -209,10 +200,13 @@
     def masked(m, d, n):
         return (m[...].astype(F32) * factor_ref[2 * d + n : 2 * d + n + 1, :]).astype(BF16)
 
-    q, g = stack_heads(q2), masked(m2, 2, 0)
-    keys = [dot(ds2[n * half : (n + 1) * half, :], q, 1, 0) for n in range(2)]
-    values = [dot(w2[n * half : (n + 1) * half, :], g, 1, 1) for n in range(2)]
+    keys, values = [None, None], [None, None]
+
+    def plus(total, part):
+        return part if total is None else total + part
+
     for d, q_ref, m, ws, x, out in (
+        (2, q2, m2, (w2, w2), x2, dq2),
         (1, q1, m1, (w1a, w1b), x1, dq1),
         (3, q3, m3, (w3, w3), x3, dq3),
         (0, q0, m0, (w0a, w0b), x0, dq0),
@@ -232,10 +226,10 @@
                 dkr_ref[...] = (dot(ds, q, 1, 0) * scale).astype(BF16)
                 grad = dot(kr[...], ds, 0, 0)
             here = slice(n * half, (n + 1) * half)
-            weights = w[here, :] if w is w3 else w[skip : skip + half, :]
+            weights = w[here, :] if w is w3 or w is w2 else w[skip : skip + half, :]
             ds = weights * ((x[here, :] - delta) * factor).astype(BF16)
-            values[n] = values[n] + dot(weights, g, 1, 1)
-            keys[n] = keys[n] + dot(ds, q, 1, 0)
+            values[n] = plus(values[n], dot(weights, g, 1, 1))
+            keys[n] = plus(keys[n], dot(ds, q, 1, 0))
             part = dot(plane_keys[here, :], ds, 0, 0)
             grad = part if grad is None else grad + part
         turn_back(grad, out)
@@ -332,18 +326,14 @@
     x0, x1, x2, x3, xr = call(
         product_kernel, "product", [square_wide] * 4 + [((rows, wide), F32)],
         (stat, *pieces, vr, m0, m1, m2, m3), 12, flops=4 * unit)
-    factors, delta, dq2, ds2 = call(
-        remote_kernel, "remote",
-        [((2 * SIDE, wide), F32), ((SIDE, wide), F32), flat, square],
-        (*all_stats, high, *pieces, w2, x2), 12, flops=unit)
-    back2 = send(dq2, shift_y(-2))
-    dq0, dq1, dq3, dkr, dvr, o0, o1, o3, o2 = call(
-        local_kernel, "local", [flat] * 3 + [small, small] + [both] * 4,
-        (factors, delta, *pieces, kr, w0a, w0b, w1a, w1b, w2, w3, x0, x1, x3, xr, ds2,
-         m0, m1, m2, m3, q0, q1, q2, q3), 16, flops=11 * unit)
-    dq1, unused = lax.optimization_barrier((dq1, back2))
+    dq0, dq1, dq2, dq3, dkr, dvr, o0, o1, o3, o2 = call(
+        local_kernel, "local", [flat] * 4 + [small, small] + [both] * 4,
+        (*all_stats, high, *pieces, kr, w0a, w0b, w1a, w1b, w2, w3, x0, x1, x2, x3, xr,
+         m0, m1, m2, m3, q0, q1, q2, q3), 16,
+        [pltpu.VMEM((2 * SIDE, wide), F32), pltpu.VMEM((SIDE, wide), F32)], flops=12 * unit)
+    returned = [send(x, shift_y(-d)) for d, x in ((2, dq2), (1, dq1), (3, dq3))]
+    o3, unused = lax.optimization_barrier((o3, returned[0]))
     total = combine(o0, [send(x, shift_z(-d)) for d, x in ((2, o2), (1, o1), (3, o3))])
-    returned = [send(x, shift_y(-d)) for d, x in ((1, dq1), (3, dq3))] + [back2]
     grad_queries = combine(dq0, returned)
     return grad_queries, total[:part], total[part:], dkr, dvr
 

time: 60.2 us -> 59.7 us (level)
  the two profiles are of different devices: /device:TPU:40 before, /device:TPU:2 now
where the time goes in v4:
time: 59.7 us; the launch traced here: 59.6 us
  starting transfers between devices  28 us (47%)
  Pallas kernels  18.4 us (31%)
  waiting for transfers between devices  10.2 us (17%)
  between operations  1.38 us (2%)
  other arithmetic  0.94 us (2%)
  local copies, waits for them, and re-layouts  0.66 us (1%)
    ppermute x18, starting transfers between devices, send(): return lax.ppermute(x, 'resp', perm)  28 us
    pallas_call x6, Pallas kernels, call(): pl.pallas_call(kernel, out_shape=[jax.ShapeDtypeStruct(*o) for o in outs]...  18.4 us
    ppermute x18, waiting for transfers between devices, send(): return lax.ppermute(x, 'resp', perm)  10.2 us
  transfers between devices with their start and end apart: 18, of which 7 were waited for; matrix products, arithmetic and copies ran while one was open for 1% of the time, Pallas kernels for 18%

profile of v4, /device:TPU:2, one launch (start us, length us, event | category | flops | bytes accessed | tf_op | source)
XLA Modules:
  0.0 59.6 jit_solution(10611957421487444452)
XLA Ops:
  0.6 1.7 %collective-permute-start = (bf16[128,1024]{1,0:T(8,128)(2,1)}, bf16[128,1024]{1,0:T(8,128)(2,1)S(1)}, u32[]{:S(2)}, u32[]{:S(2)}) collective-permute-start(bf16[128,1024]{1,0:T(8,128)(2,1)} %q_hbm.1), channel_id=1, source_target_pairs={{0,32},{8,40},{16,48},{24,56},{32,64},{40,72},{48,80},{56,88},{64,... | collective-permute-start | bytes 786440 | tf_op jit(solution)/shard_map/ppermute | solution.py:253
  2.9 1.2 %prepare.1 = (bf16[128,1024]{1,0:T(8,128)(2,1)S(1)}, bf16[128,1024]{1,0:T(8,128)(2,1)S(1)}, bf16[512,128]{1,0:T(8,128)(2,1)S(1)}, bf16[128,128]{1,0:T(8,128)(2,1)S(1)}, bf16[128,128]{1,0:T(8,128)(2,1)S(1)}) custom-call(s32[1]{0:T(128)S(6)} %copy.12.len_hbm, bf16[128,1024]{1,0:T(8,128)(2,1)} %q_hbm.1, bf16[128,1024]{1,0:T(8,128)(2,1)} %g_hbm.1, ...), custom_call_target="tpu_custom_call" | custom-call | bytes 1048576 | tf_op jit(solution)/shard_map/prepare/pallas_call | solution.py:269
  4.1 2.0 %collective-permute-start.1 = (bf16[512,128]{1,0:T(8,128)(2,1)S(1)}, bf16[512,128]{1,0:T(8,128)(2,1)S(1)}, u32[]{:S(2)}, u32[]{:S(2)}) collective-permute-start(bf16[512,128]{1,0:T(8,128)(2,1)S(1)} %get-tuple-element.48.p0), channel_id=1, source_target_pairs={{0,8},{8,16},{16,24},{24,0},{32,40},{40,48},{48,56},{56,32},{64,72... | collective-permute-start | bytes 393224 | tf_op jit(solution)/shard_map/ppermute | solution.py:253
  6.1 1.7 %collective-permute-start.7 = (bf16[128,1024]{1,0:T(8,128)(2,1)S(1)}, bf16[128,1024]{1,0:T(8,128)(2,1)S(1)}, u32[]{:S(2)}, u32[]{:S(2)}) collective-permute-start(bf16[128,1024]{1,0:T(8,128)(2,1)S(1)} %get-tuple-element.60.m0), channel_id=1, source_target_pairs={{0,96},{8,104},{16,112},{24,120},{32,0},{40,8},{48,16},{56,24},{64... | collective-permute-start | bytes 786440 | tf_op jit(solution)/shard_map/ppermute | solution.py:253
  7.8 1.8 %collective-permute-start.3 = (bf16[128,1024]{1,0:T(8,128)(2,1)}, bf16[128,1024]{1,0:T(8,128)(2,1)S(1)}, u32[]{:S(2)}, u32[]{:S(2)}) collective-permute-start(bf16[128,1024]{1,0:T(8,128)(2,1)} %q_hbm.1), channel_id=1, source_target_pairs={{0,96},{8,104},{16,112},{24,120},{32,0},{40,8},{48,16},{56,24},{64... | collective-permute-start | bytes 786440 | tf_op jit(solution)/shard_map/ppermute | solution.py:253
  9.6 2.8 %collective-permute-start.4 = (bf16[512,128]{1,0:T(8,128)(2,1)S(1)}, bf16[512,128]{1,0:T(8,128)(2,1)S(1)}, u32[]{:S(2)}, u32[]{:S(2)}) collective-permute-start(bf16[512,128]{1,0:T(8,128)(2,1)S(1)} %get-tuple-element.48.p0), channel_id=1, source_target_pairs={{0,24},{8,0},{16,8},{24,16},{32,56},{40,32},{48,40},{56,48},{64,88... | collective-permute-start | bytes 393224 | tf_op jit(solution)/shard_map/ppermute | solution.py:253
  12.4 0.0 collective-permute-done.1.p1
  12.4 0.0 collective-permute-done.q1
  12.4 1.4 %collective-permute-start.2 = (bf16[128,1024]{1,0:T(8,128)(2,1)S(1)}, bf16[128,1024]{1,0:T(8,128)(2,1)S(1)}, u32[]{:S(2)}, u32[]{:S(2)}) collective-permute-start(bf16[128,1024]{1,0:T(8,128)(2,1)S(1)} %collective-permute-done.q1), channel_id=1, source_target_pairs={{0,32},{8,40},{16,48},{24,56},{32,64},{40,72},{48,80},{56,88},{64,... | collective-permute-start | bytes 786440 | tf_op jit(solution)/shard_map/ppermute | solution.py:253
  13.8 1.1 %collective-permute-done.4.p3 = bf16[512,128]{1,0:T(8,128)(2,1)S(1)} collective-permute-done((bf16[512,128]{1,0:T(8,128)(2,1)S(1)}, bf16[512,128]{1,0:T(8,128)(2,1)S(1)}, u32[]{:S(2)}, u32[]{:S(2)}) %collective-permute-start.4) | collective-permute-done | bytes 131104 | tf_op jit(solution)/shard_map/ppermute | solution.py:253
  14.9 4.2 %collective-permute-start.5 = (bf16[512,128]{1,0:T(8,128)(2,1)S(1)}, bf16[512,128]{1,0:T(8,128)(2,1)S(1)}, u32[]{:S(2)}, u32[]{:S(2)}) collective-permute-start(bf16[512,128]{1,0:T(8,128)(2,1)S(1)} %collective-permute-done.4.p3), channel_id=1, source_target_pairs={{0,24},{8,0},{16,8},{24,16},{32,56},{40,32},{48,40},{56,48},{64,88... | collective-permute-start | bytes 393224 | tf_op jit(solution)/shard_map/ppermute | solution.py:253
  19.1 0.2 collective-permute-start.6
  19.4 0.0 collective-permute-done.7.m3
  19.4 3.0 %collective-permute-start.8 = (bf16[128,1024]{1,0:T(8,128)(2,1)S(1)}, bf16[128,1024]{1,0:T(8,128)(2,1)S(1)}, u32[]{:S(2)}, u32[]{:S(2)}) collective-permute-start(bf16[128,1024]{1,0:T(8,128)(2,1)S(1)} %collective-permute-done.7.m3), channel_id=1, source_target_pairs={{0,96},{8,104},{16,112},{24,120},{32,0},{40,8},{48,16},{56,24},{64... | collective-permute-start | bytes 786440 | tf_op jit(solution)/shard_map/ppermute | solution.py:253
  22.4 2.1 %first.1 = (bf16[640,1024]{1,0:T(8,128)(2,1)S(1)}, bf16[512,1024]{1,0:T(8,128)(2,1)S(1)}, f32[2,1024]{1,0:T(2,128)S(1)}, f32[2,1024]{1,0:T(2,128)S(1)}, f32[128,...) custom-call(bf16[128,1024]{1,0:T(8,128)(2,1)S(1)} %get-tuple-element.45.q0, bf16[128,1024]{1,0:T(8,128)(2,1)S(1)} %collective-permute-done.q1, ...), custom_call_target="tpu_custom_call" | custom-call | flops 805306368 | bytes 1048576 | tf_op jit(solution)/shard_map/first/pallas_call | solution.py:269
  24.5 0.0 collective-permute-done.3.q3
  24.5 0.0 collective-permute-done.5.p2
  24.5 0.0 collective-permute-done.2.q2
  24.5 5.3 %second.1 = (bf16[512,1024]{1,0:T(8,128)(2,1)S(1)}, bf16[512,1024]{1,0:T(8,128)(2,1)S(1)}, bf16[1024,1024]{1,0:T(8,128)(2,1)S(1)}, bf16[1024,1024]{1,0:T(8,128)(...) custom-call(bf16[128,1024]{1,0:T(8,128)(2,1)S(1)} %get-tuple-element, ...), custom_call_target="tpu_custom_call" | custom-call | flops 1610612736 | bytes 1048576 | tf_op jit(solution)/shard_map/second/pallas_call | solution.py:269
  29.8 0.0 collective-permute-done.6.m1
  29.9 0.0 collective-permute-done.8.m2
  29.9 0.6 %delta.1 = (f32[8,1024]{1,0:T(8,128)S(1)}, f32[8,1024]{1,0:T(8,128)S(1)}) custom-call(f32[2,1024]{1,0:T(2,128)S(1)} %get-tuple-element.49.high01, f32[4,1024]{1,0:T(4,128)S(1)} %get-tuple-element.51.highs, f32[2,1024]{1,0:T(2,128)S(1)} %get-tuple-element.52.lse01, f32[4,1024]{1,0:T(4,128)S(1)} %get-tuple-element.53.lses, ...), custom_call_target="tpu_custom_call" | custom-call | flops 134217728 | bytes 1048576 | tf_op jit(solution)/shard_map/delta/pallas_call | solution.py:269
  30.5 0.2 collective-permute-start.11
  30.7 1.0 %collective-permute-start.10 = (f32[8,1024]{1,0:T(8,128)S(1)}, f32[8,1024]{1,0:T(8,128)S(1)}, u32[]{:S(2)}, u32[]{:S(2)}) collective-permute-start(f32[8,1024]{1,0:T(8,128)S(1)} %get-tuple-element.61.stat_ref.t0), channel_id=1, source_target_pairs={{0,64},{8,72},{16,80},{24,88},{32,96},{40,104},{48,112},{56,120},{... | collective-permute-start | bytes 98312 | tf_op jit(solution)/shard_map/ppermute | solution.py:253
  31.7 0.9 %collective-permute-start.9 = (f32[8,1024]{1,0:T(8,128)S(1)}, f32[8,1024]{1,0:T(8,128)S(1)}, u32[]{:S(2)}, u32[]{:S(2)}) collective-permute-start(f32[8,1024]{1,0:T(8,128)S(1)} %get-tuple-element.61.stat_ref.t0), channel_id=1, source_target_pairs={{0,32},{8,40},{16,48},{24,56},{32,64},{40,72},{48,80},{56,88},{64,... | collective-permute-start | bytes 98312 | tf_op jit(solution)/shard_map/ppermute | solution.py:253
  32.6 2.4 %product.1 = (f32[1024,1024]{1,0:T(8,128)S(1)}, f32[1024,1024]{1,0:T(8,128)S(1)}, f32[1024,1024]{1,0:T(8,128)S(1)}, f32[1024,1024]{1,0:T(8,128)S(1)}, f32[128,1024]{1,0:T(8,128)S(1)}) custom-call(f32[8,1024]{1,0:T(8,128)S(1)} %get-tuple-element.61.stat_ref.t0, bf16[512,128]{1,0:T(8,128)(2,1)S(1)} %get-tuple-element.48.p0, ...), custom_call_target="tpu_custom_call" | custom-call | flops 1073741824 | bytes 1048576 | tf_op jit(solution)/shard_map/product/pallas_call | solution.py:269
  35.0 0.0 collective-permute-done.11.t3
  35.0 1.1 %collective-permute-done.10.t2 = f32[8,1024]{1,0:T(8,128)S(1)} collective-permute-done((f32[8,1024]{1,0:T(8,128)S(1)}, f32[8,1024]{1,0:T(8,128)S(1)}, u32[]{:S(2)}, u32[]{:S(2)}) %collective-permute-start.10) | collective-permute-done | bytes 32800 | tf_op jit(solution)/shard_map/ppermute | solution.py:253
  36.1 1.1 %collective-permute-done.9.t1 = f32[8,1024]{1,0:T(8,128)S(1)} collective-permute-done((f32[8,1024]{1,0:T(8,128)S(1)}, f32[8,1024]{1,0:T(8,128)S(1)}, u32[]{:S(2)}, u32[]{:S(2)}) %collective-permute-start.9) | collective-permute-done | bytes 32800 | tf_op jit(solution)/shard_map/ppermute | solution.py:253
  37.2 6.8 %local.1 = (bf16[128,1024]{1,0:T(8,128)(2,1)S(1)}, bf16[128,1024]{1,0:T(8,128)(2,1)S(1)}, bf16[128,1024]{1,0:T(8,128)(2,1)S(1)}, bf16[128,1024]{1,0:T(8,128)(2,1...) custom-call(f32[8,1024]{1,0:T(8,128)S(1)} %get-tuple-element.61.stat, ...), custom_call_target="tpu_custom_call" | custom-call | flops 3221225472 | bytes 1048576 | tf_op jit(solution)/shard_map/local/pallas_call | solution.py:269
  44.0 2.1 %collective-permute-start.12 = (bf16[128,1024]{1,0:T(8,128)(2,1)S(1)}, bf16[128,1024]{1,0:T(8,128)(2,1)S(1)}, u32[]{:S(2)}, u32[]{:S(2)}) collective-permute-start(bf16[128,1024]{1,0:T(8,128)(2,1)S(1)} %get-tuple-element.75), channel_id=1, source_target_pairs={{0,64},{8,72},{16,80},{24,88},{32,96},{40,104},{48,112},{56,120},{... | collective-permute-start | bytes 786440 | tf_op jit(solution)/shard_map/ppermute | solution.py:253
  46.0 1.5 %collective-permute-start.13 = (bf16[128,1024]{1,0:T(8,128)(2,1)S(1)}, bf16[128,1024]{1,0:T(8,128)(2,1)S(1)}, u32[]{:S(2)}, u32[]{:S(2)}) collective-permute-start(bf16[128,1024]{1,0:T(8,128)(2,1)S(1)} %get-tuple-element.76), channel_id=1, source_target_pairs={{0,96},{8,104},{16,112},{24,120},{32,0},{40,8},{48,16},{56,24},{64... | collective-permute-start | bytes 786440 | tf_op jit(solution)/shard_map/ppermute | solution.py:253
  47.5 0.5 collective-permute-start.14
  48.0 1.4 %collective-permute-start.15 = (bf16[512,128]{1,0:T(8,128)(2,1)S(1)}, bf16[512,128]{1,0:T(8,128)(2,1)S(1)}, u32[]{:S(2)}, u32[]{:S(2)}) collective-permute-start(bf16[512,128]{1,0:T(8,128)(2,1)S(1)} %get-tuple-element.79), channel_id=1, source_target_pairs={{0,16},{8,24},{16,0},{24,8},{32,48},{40,56},{48,32},{56,40},{64,80... | collective-permute-start | bytes 393224 | tf_op jit(solution)/shard_map/ppermute | solution.py:253
  49.4 1.0 %collective-permute-start.16 = (bf16[512,128]{1,0:T(8,128)(2,1)S(1)}, bf16[512,128]{1,0:T(8,128)(2,1)S(1)}, u32[]{:S(2)}, u32[]{:S(2)}) collective-permute-start(bf16[512,128]{1,0:T(8,128)(2,1)S(1)} %get-tuple-element.80), channel_id=1, source_target_pairs={{0,24},{8,0},{16,8},{24,16},{32,56},{40,32},{48,40},{56,48},{64,88... | collective-permute-start | bytes 393224 | tf_op jit(solution)/shard_map/ppermute | solution.py:253
  50.4 1.6 %collective-permute-done.12 = bf16[128,1024]{1,0:T(8,128)(2,1)S(1)} collective-permute-done((bf16[128,1024]{1,0:T(8,128)(2,1)S(1)}, bf16[128,1024]{1,0:T(8,128)(2,1)S(1)}, u32[]{:S(2)}, u32[]{:S(2)}) %collective-permute-start.12) | collective-permute-done | bytes 262176 | tf_op jit(solution)/shard_map/ppermute | solution.py:253
  52.1 0.6 %collective-permute-start.17 = (bf16[512,128]{1,0:T(8,128)(2,1)S(1)}, bf16[512,128]{1,0:T(8,128)(2,1)S(1)}, u32[]{:S(2)}, u32[]{:S(2)}) collective-permute-start(bf16[512,128]{1,0:T(8,128)(2,1)S(1)} %get-tuple-element.82), channel_id=1, source_target_pairs={{0,8},{8,16},{16,24},{24,0},{32,40},{40,48},{48,56},{56,32},{64,72... | collective-permute-start | bytes 393224 | tf_op jit(solution)/shard_map/ppermute | solution.py:253
  52.7 1.3 %collective-permute-done.13 = bf16[128,1024]{1,0:T(8,128)(2,1)S(1)} collective-permute-done((bf16[128,1024]{1,0:T(8,128)(2,1)S(1)}, bf16[128,1024]{1,0:T(8,128)(2,1)S(1)}, u32[]{:S(2)}, u32[]{:S(2)}) %collective-permute-start.13) | collective-permute-done | bytes 262176 | tf_op jit(solution)/shard_map/ppermute | solution.py:253
  54.0 1.1 %collective-permute-done.14 = bf16[128,1024]{1,0:T(8,128)(2,1)S(1)} collective-permute-done((bf16[128,1024]{1,0:T(8,128)(2,1)S(1)}, bf16[128,1024]{1,0:T(8,128)(2,1)S(1)}, u32[]{:S(2)}, u32[]{:S(2)}) %collective-permute-start.14) | collective-permute-done | bytes 262176 | tf_op jit(solution)/shard_map/ppermute | solution.py:253
  55.1 0.9 %add_convert_fusion = bf16[128,1024]{1,0:T(8,128)(2,1)} fusion(bf16[128,1024]{1,0:T(8,128)(2,1)S(1)} %collective-permute-done.14, bf16[128,1024]{1,0:T(8,128)(2,1)S(1)} %collective-permute-done.13, bf16[128,1024]{1,0:T(8,128)(2,1)S(1)} %collective-permute-done.12, bf16[128,1024]{1,0:T(8,128)(2,1)S(1)} %get-tuple-element.74), kind=kLoop, calls=%fused_computation | loop fusion | flops 1048576 | bytes 1310720 | tf_op jit(solution)/shard_map/convert_element_type | solution.py:260
  55.9 0.0 collective-permute-done.15
  55.9 0.0 collective-permute-done.16
  56.0 2.9 %collective-permute-done.17 = bf16[512,128]{1,0:T(8,128)(2,1)S(1)} collective-permute-done((bf16[512,128]{1,0:T(8,128)(2,1)S(1)}, bf16[512,128]{1,0:T(8,128)(2,1)S(1)}, u32[]{:S(2)}, u32[]{:S(2)}) %collective-permute-start.17) | collective-permute-done | bytes 131104 | tf_op jit(solution)/shard_map/ppermute | solution.py:253
  58.8 0.1 add_convert_fusion.1
  58.9 0.7 %fusion = (bf16[256,128]{1,0:T(8,128)(2,1)}, bf16[256,128]{1,0:T(8,128)(2,1)}) fusion(bf16[512,128]{1,0:T(8,128)(2,1)S(1)} %add_convert_fusion.1), kind=kLoop, calls=%fused_computation.2 | loop fusion | bytes 262144 | tf_op jit(solution)/shard_map/slice | solution.py:338
Async XLA Ops:
  0.6 11.7 %collective-permute-start = (bf16[128,1024]{1,0:T(8,128)(2,1)}, bf16[128,1024]{1,0:T(8,128)(2,1)S(1)}, u32[]{:S(2)}, u32[]{:S(2)}) collective-permute-start(bf16[128,1024]{1,0:T(8,128)(2,1)} %q_hbm.1), channel_id=1, source_target_pairs={{0,32},{8,40},{16,48},{24,56},{32,64},{40,72},{48,80},{56,88},{64,... | collective-permute-start | bytes 786440 | tf_op jit(solution)/shard_map/ppermute | solution.py:253
  4.1 8.3 %collective-permute-start.1 = (bf16[512,128]{1,0:T(8,128)(2,1)S(1)}, bf16[512,128]{1,0:T(8,128)(2,1)S(1)}, u32[]{:S(2)}, u32[]{:S(2)}) collective-permute-start(bf16[512,128]{1,0:T(8,128)(2,1)S(1)} %get-tuple-element.48.p0), channel_id=1, source_target_pairs={{0,8},{8,16},{16,24},{24,0},{32,40},{40,48},{48,56},{56,32},{64,72... | collective-permute-start | bytes 393224 | tf_op jit(solution)/shard_map/ppermute | solution.py:253
  6.1 13.3 %collective-permute-start.7 = (bf16[128,1024]{1,0:T(8,128)(2,1)S(1)}, bf16[128,1024]{1,0:T(8,128)(2,1)S(1)}, u32[]{:S(2)}, u32[]{:S(2)}) collective-permute-start(bf16[128,1024]{1,0:T(8,128)(2,1)S(1)} %get-tuple-element.60.m0), channel_id=1, source_target_pairs={{0,96},{8,104},{16,112},{24,120},{32,0},{40,8},{48,16},{56,24},{64... | collective-permute-start | bytes 786440 | tf_op jit(solution)/shard_map/ppermute | solution.py:253
  7.8 16.7 %collective-permute-start.3 = (bf16[128,1024]{1,0:T(8,128)(2,1)}, bf16[128,1024]{1,0:T(8,128)(2,1)S(1)}, u32[]{:S(2)}, u32[]{:S(2)}) collective-permute-start(bf16[128,1024]{1,0:T(8,128)(2,1)} %q_hbm.1), channel_id=1, source_target_pairs={{0,96},{8,104},{16,112},{24,120},{32,0},{40,8},{48,16},{56,24},{64... | collective-permute-start | bytes 786440 | tf_op jit(solution)/shard_map/ppermute | solution.py:253
  9.6 5.3 %collective-permute-start.4 = (bf16[512,128]{1,0:T(8,128)(2,1)S(1)}, bf16[512,128]{1,0:T(8,128)(2,1)S(1)}, u32[]{:S(2)}, u32[]{:S(2)}) collective-permute-start(bf16[512,128]{1,0:T(8,128)(2,1)S(1)} %get-tuple-element.48.p0), channel_id=1, source_target_pairs={{0,24},{8,0},{16,8},{24,16},{32,56},{40,32},{48,40},{56,48},{64,88... | collective-permute-start | bytes 393224 | tf_op jit(solution)/shard_map/ppermute | solution.py:253
  12.4 12.1 %collective-permute-start.2 = (bf16[128,1024]{1,0:T(8,128)(2,1)S(1)}, bf16[128,1024]{1,0:T(8,128)(2,1)S(1)}, u32[]{:S(2)}, u32[]{:S(2)}) collective-permute-start(bf16[128,1024]{1,0:T(8,128)(2,1)S(1)} %collective-permute-done.q1), channel_id=1, source_target_pairs={{0,32},{8,40},{16,48},{24,56},{32,64},{40,72},{48,80},{56,88},{64,... | collective-permute-start | bytes 786440 | tf_op jit(solution)/shard_map/ppermute | solution.py:253
  14.9 9.6 %collective-permute-start.5 = (bf16[512,128]{1,0:T(8,128)(2,1)S(1)}, bf16[512,128]{1,0:T(8,128)(2,1)S(1)}, u32[]{:S(2)}, u32[]{:S(2)}) collective-permute-start(bf16[512,128]{1,0:T(8,128)(2,1)S(1)} %collective-permute-done.4.p3), channel_id=1, source_target_pairs={{0,24},{8,0},{16,8},{24,16},{32,56},{40,32},{48,40},{56,48},{64,88... | collective-permute-start | bytes 393224 | tf_op jit(solution)/shard_map/ppermute | solution.py:253
  19.1 10.7 %collective-permute-start.6 = (bf16[128,1024]{1,0:T(8,128)(2,1)S(1)}, bf16[128,1024]{1,0:T(8,128)(2,1)S(1)}, u32[]{:S(2)}, u32[]{:S(2)}) collective-permute-start(bf16[128,1024]{1,0:T(8,128)(2,1)S(1)} %get-tuple-element.60.m0), channel_id=1, source_target_pairs={{0,32},{8,40},{16,48},{24,56},{32,64},{40,72},{48,80},{56,88},{64,... | collective-permute-start | bytes 786440 | tf_op jit(solution)/shard_map/ppermute | solution.py:253
  19.4 10.5 %collective-permute-start.8 = (bf16[128,1024]{1,0:T(8,128)(2,1)S(1)}, bf16[128,1024]{1,0:T(8,128)(2,1)S(1)}, u32[]{:S(2)}, u32[]{:S(2)}) collective-permute-start(bf16[128,1024]{1,0:T(8,128)(2,1)S(1)} %collective-permute-done.7.m3), channel_id=1, source_target_pairs={{0,96},{8,104},{16,112},{24,120},{32,0},{40,8},{48,16},{56,24},{64... | collective-permute-start | bytes 786440 | tf_op jit(solution)/shard_map/ppermute | solution.py:253
  30.5 4.5 %collective-permute-start.11 = (f32[8,1024]{1,0:T(8,128)S(1)}, f32[8,1024]{1,0:T(8,128)S(1)}, u32[]{:S(2)}, u32[]{:S(2)}) collective-permute-start(f32[8,1024]{1,0:T(8,128)S(1)} %get-tuple-element.61.stat_ref.t0), channel_id=1, source_target_pairs={{0,96},{8,104},{16,112},{24,120},{32,0},{40,8},{48,16},{56,24},{64... | collective-permute-start | bytes 98312 | tf_op jit(solution)/shard_map/ppermute | solution.py:253
  30.7 5.4 %collective-permute-start.10 = (f32[8,1024]{1,0:T(8,128)S(1)}, f32[8,1024]{1,0:T(8,128)S(1)}, u32[]{:S(2)}, u32[]{:S(2)}) collective-permute-start(f32[8,1024]{1,0:T(8,128)S(1)} %get-tuple-element.61.stat_ref.t0), channel_id=1, source_target_pairs={{0,64},{8,72},{16,80},{24,88},{32,96},{40,104},{48,112},{56,120},{... | collective-permute-start | bytes 98312 | tf_op jit(solution)/shard_map/ppermute | solution.py:253
  31.7 5.5 %collective-permute-start.9 = (f32[8,1024]{1,0:T(8,128)S(1)}, f32[8,1024]{1,0:T(8,128)S(1)}, u32[]{:S(2)}, u32[]{:S(2)}) collective-permute-start(f32[8,1024]{1,0:T(8,128)S(1)} %get-tuple-element.61.stat_ref.t0), channel_id=1, source_target_pairs={{0,32},{8,40},{16,48},{24,56},{32,64},{40,72},{48,80},{56,88},{64,... | collective-permute-start | bytes 98312 | tf_op jit(solution)/shard_map/ppermute | solution.py:253
  44.0 8.1 %collective-permute-start.12 = (bf16[128,1024]{1,0:T(8,128)(2,1)S(1)}, bf16[128,1024]{1,0:T(8,128)(2,1)S(1)}, u32[]{:S(2)}, u32[]{:S(2)}) collective-permute-start(bf16[128,1024]{1,0:T(8,128)(2,1)S(1)} %get-tuple-element.75), channel_id=1, source_target_pairs={{0,64},{8,72},{16,80},{24,88},{32,96},{40,104},{48,112},{56,120},{... | collective-permute-start | bytes 786440 | tf_op jit(solution)/shard_map/ppermute | solution.py:253
  46.0 8.0 %collective-permute-start.13 = (bf16[128,1024]{1,0:T(8,128)(2,1)S(1)}, bf16[128,1024]{1,0:T(8,128)(2,1)S(1)}, u32[]{:S(2)}, u32[]{:S(2)}) collective-permute-start(bf16[128,1024]{1,0:T(8,128)(2,1)S(1)} %get-tuple-element.76), channel_id=1, source_target_pairs={{0,96},{8,104},{16,112},{24,120},{32,0},{40,8},{48,16},{56,24},{64... | collective-permute-start | bytes 786440 | tf_op jit(solution)/shard_map/ppermute | solution.py:253
  47.5 7.6 %collective-permute-start.14 = (bf16[128,1024]{1,0:T(8,128)(2,1)S(1)}, bf16[128,1024]{1,0:T(8,128)(2,1)S(1)}, u32[]{:S(2)}, u32[]{:S(2)}) collective-permute-start(bf16[128,1024]{1,0:T(8,128)(2,1)S(1)} %get-tuple-element.77), channel_id=1, source_target_pairs={{0,32},{8,40},{16,48},{24,56},{32,64},{40,72},{48,80},{56,88},{64,... | collective-permute-start | bytes 786440 | tf_op jit(solution)/shard_map/ppermute | solution.py:253
  48.0 7.9 %collective-permute-start.15 = (bf16[512,128]{1,0:T(8,128)(2,1)S(1)}, bf16[512,128]{1,0:T(8,128)(2,1)S(1)}, u32[]{:S(2)}, u32[]{:S(2)}) collective-permute-start(bf16[512,128]{1,0:T(8,128)(2,1)S(1)} %get-tuple-element.79), channel_id=1, source_target_pairs={{0,16},{8,24},{16,0},{24,8},{32,48},{40,56},{48,32},{56,40},{64,80... | collective-permute-start | bytes 393224 | tf_op jit(solution)/shard_map/ppermute | solution.py:253
  49.4 6.5 %collective-permute-start.16 = (bf16[512,128]{1,0:T(8,128)(2,1)S(1)}, bf16[512,128]{1,0:T(8,128)(2,1)S(1)}, u32[]{:S(2)}, u32[]{:S(2)}) collective-permute-start(bf16[512,128]{1,0:T(8,128)(2,1)S(1)} %get-tuple-element.80), channel_id=1, source_target_pairs={{0,24},{8,0},{16,8},{24,16},{32,56},{40,32},{48,40},{56,48},{64,88... | collective-permute-start | bytes 393224 | tf_op jit(solution)/shard_map/ppermute | solution.py:253
  52.1 6.8 %collective-permute-start.17 = (bf16[512,128]{1,0:T(8,128)(2,1)S(1)}, bf16[512,128]{1,0:T(8,128)(2,1)S(1)}, u32[]{:S(2)}, u32[]{:S(2)}) collective-permute-start(bf16[512,128]{1,0:T(8,128)(2,1)S(1)} %get-tuple-element.82), channel_id=1, source_target_pairs={{0,8},{8,16},{16,24},{24,0},{32,40},{40,48},{48,56},{56,32},{64,72... | collective-permute-start | bytes 393224 | tf_op jit(solution)/shard_map/ppermute | solution.py:253
